TPU v7x, 128 devices: a whole 4x4x4 slice. The times are simulated.
128 devices in a mesh: band: 2 (over x_lo), dom: 64 (over x_hi, y, z, core).
Axes of the slice: x: 4 (x_hi: 2, x_lo: 2; x = x_hi * 2 + x_lo), y: 4, z: 4, core: 2. Of those that a mesh axis runs over, the one named last changes fastest.
Arguments:
- orbitals: float32 [48, 64, 12, 2304], P('band', 'dom'), as said below
- potential: float32 [64, 12, 2304], P('dom'), may hold values from -1.5 to 1.5
Outputs:
- rotated: float32 [48, 64, 12, 2304], P('band', 'dom')
Inputs may be any that keep to these rules, and one draw needn't show every extreme that they name: `orbitals`: orbitals are linearly independent.
All inputs are finite; a program needn't handle non-finite values.
Results may differ from a plain program's by a relative error of at most 0.00023.
Values sent between devices are 32-bit elements; how exact they have to be, the bound alone decides.
A program may use at most 128 MiB of HBM per device.

v0:
```python
import jax
import jax.numpy as jnp
from jax import lax
from jax.sharding import PartitionSpec as P

CX = 12
CY = 48
CZ = 48


stencil_weights = (
    -5369.0 / 1800.0,
    12.0 / 7.0,
    -15.0 / 56.0,
    10.0 / 189.0,
    -1.0 / 112.0,
    2.0 / 1925.0,
    -1.0 / 16632.0,
)
centre_shift = 7.25
half_width = 5.25


def swapped(value, axis, apart):
    return lax.ppermute(value, axis, [(i, i ^ 1 << apart) for i in range(lax.axis_size(axis))])


def padded_along(field, dim, first_bit, brick):
    extent = field.shape[dim]
    low_face = lax.slice_in_dim(field, 0, 6, axis=dim)
    high_face = lax.slice_in_dim(field, extent - 6, extent, axis=dim)
    code = brick // (1 << first_bit) % 4
    coord = jnp.bitwise_xor(code, code // 2)
    odd = coord % 2 == 1
    received = []
    for bit in range(2):
        outgoing = jnp.where(odd == (bit == 1), high_face, low_face)
        received.append(swapped(outgoing, "dom", first_bit + bit))
    lower_rim = jnp.where(odd, received[0], received[1])
    upper_rim = jnp.where(odd, received[1], received[0])
    return jnp.concatenate([lower_rim, field, upper_rim], dim)


def apply_h(field, pot):
    brick = lax.axis_index("dom")
    wide_x = padded_along(field, 1, 0, brick)
    wide_y = padded_along(field, 2, 2, brick)
    wide_z = padded_along(field, 3, 4, brick)
    size_x, size_y, size_z = (field.shape[1], field.shape[2], field.shape[3])
    laplace = 3.0 * stencil_weights[0] * field
    for shift in range(1, 7):
        near = wide_x[:, 6 + shift : 6 + shift + size_x] + wide_x[:, 6 - shift : 6 - shift + size_x]
        near = (
            near
            + wide_y[:, :, 6 + shift : 6 + shift + size_y]
            + wide_y[:, :, 6 - shift : 6 - shift + size_y]
        )
        near = (
            near
            + wide_z[:, :, :, 6 + shift : 6 + shift + size_z]
            + wide_z[:, :, :, 6 - shift : 6 - shift + size_z]
        )
        laplace = laplace + stencil_weights[shift] * near
    return -0.5 * laplace + pot * field


def body(orbitals, potential):
    group_orb = orbitals.shape[0]
    field = orbitals.reshape(group_orb, CX, CY, CZ)
    pot = potential.reshape(CX, CY, CZ)
    first = (apply_h(field, pot) - centre_shift * field) / half_width
    filtered = 2.0 * (apply_h(first, pot) - centre_shift * first) / half_width - field
    own_flat = filtered.reshape(group_orb, -1)
    total_orb = group_orb * lax.axis_size("band")
    scale = 1.0 / (own_flat.shape[1] * lax.axis_size("dom"))
    offset = lax.axis_index("band") * group_orb
    every = lax.all_gather(own_flat, "band", axis=0, tiled=True)
    gram = jnp.dot(every, every.T, precision=lax.Precision.HIGHEST)
    gram = lax.psum(gram, "dom") * scale
    lower = jnp.linalg.cholesky(gram)
    inverse = lax.linalg.triangular_solve(
        lower, jnp.eye(total_orb, dtype=jnp.float32), left_side=True, lower=True
    )
    block_rows = lax.dynamic_slice_in_dim(inverse, offset, group_orb, 0)
    rotated = jnp.dot(block_rows, every, precision=lax.Precision.HIGHEST)
    return rotated.reshape(orbitals.shape)


def solution(mesh):
    return jax.shard_map(
        body,
        mesh=mesh,
        in_specs=(P("band", "dom", None, None), P("dom", None, None)),
        out_specs=P("band", "dom", None, None),
        check_vma=False,
    )
```

profile of v0, /device:TPU:2, one launch (start us, length us, event | category | flops | bytes accessed | tf_op | source)
XLA Modules:
  0.0 994.2 jit_solution(15568436078676677417)
XLA Ops:
  8.8 5.8 reshape.19
  24.2 12.1 %slice_select_fusion.3 = (f32[24,12,48,6]{3,2,0,1:T(8,128)}, f32[24,12,48,6]{3,2,0,1:T(8,128)}) fusion(f32[24,12,48,48]{3,2,0,1:T(8,128)} %reshape.19, pred[]{:T(512)S(6)} %eq.42, pred[]{:T(512)S(6)} %eq.43), kind=kLoop, calls=%fused_computation.263 | loop fusion | flops 165888 | bytes 1327106 | tf_op jit(solution)/shard_map/jit(_where)/select_n | solution.py:37
  36.3 5.8 copy.32
  45.0 5.8 copy.31
  52.9 5.5 slice_select_fusion.7
  59.4 13.8 %collective-permute-done.4 = f32[24,12,48,6]{2,0,3,1:T(8,128)} collective-permute-done((f32[24,12,48,6]{2,0,3,1:T(8,128)}, f32[24,12,48,6]{2,0,3,1:T(8,128)}, u32[]{:S(2)}, u32[]{:S(2)}) %collective-permute-start.4) | collective-permute-done | bytes 331808 | tf_op jit(solution)/shard_map/ppermute | solution.py:25
  91.3 11.4 %broadcast_select_fusion.3 = (f32[24,12,48,6]{3,2,0,1:T(8,128)}, f32[24,12,48,6]{3,2,0,1:T(8,128)}) fusion(f32[24,12,48,6]{3,2,0,1:T(8,128)} %copy.33, f32[24,12,48,6]{3,2,0,1:T(8,128)} %copy.34, pred[]{:T(512)S(6)} %eq.42), kind=kLoop, calls=%fused_computation.268 | loop fusion | flops 165888 | bytes 1327105 | tf_op jit(solution)/shard_map/jit(_where)/select_n | solution.py:40
  102.7 33.1 %collective-permute-done = f32[24,6,48,48]{3,2,0,1:T(8,128)} collective-permute-done((f32[24,6,48,48]{3,2,0,1:T(8,128)}, f32[24,6,48,48]{3,2,0,1:T(8,128)}, u32[]{:S(2)}, u32[]{:S(2)}) %collective-permute-start) | collective-permute-done | bytes 1327136 | tf_op jit(solution)/shard_map/ppermute | solution.py:25
  135.8 5.6 broadcast_select_fusion.7
  141.4 141.3 %broadcast_multiply_fusion = (f32[24,12,48,48]{3,2,0,1:T(8,128)}, f32[24,12,48,48]{3,2,0,1:T(8,128)}) fusion(f32[24,12,48,48]{3,2,0,1:T(8,128)} %reshape.19, f32[12,48,48]{2,1,0:T(8,128)} %mul.99, f32[24,12,48,6]{3,2,0,1:T(8,128)} %get-tuple-element.10, f32[24,12,48,6]{3,2,0,1:T(8,128)} %get-tuple-element.9, f32[24,12,6,48]{3,2,0,1:T(8,128)} %get-tuple-element.30, ...), kind=kLoop, calls=%fused_computation.264 | loop fusion | flops 56401920 | bytes 12054528 | tf_op jit(solution)/shard_map/div | solution.py:71
  284.6 12.2 %slice_select_fusion.1 = (f32[24,12,48,6]{3,2,0,1:T(8,128)}, f32[24,12,48,6]{3,2,0,1:T(8,128)}) fusion(f32[24,12,48,48]{3,2,0,1:T(8,128)} %get-tuple-element.5, pred[]{:T(512)S(6)} %eq.42, pred[]{:T(512)S(6)} %eq.43), kind=kLoop, calls=%fused_computation.261 | loop fusion | flops 165888 | bytes 1327106 | tf_op jit(solution)/shard_map/jit(_where)/select_n | solution.py:37
  299.5 5.8 copy.43
  305.3 5.8 copy.44
  314.0 5.5 slice_select_fusion.5
  320.6 12.4 %collective-permute-done.10 = f32[24,12,48,6]{2,0,3,1:T(8,128)S(1)} collective-permute-done((f32[24,12,48,6]{2,0,3,1:T(8,128)}, f32[24,12,48,6]{2,0,3,1:T(8,128)S(1)}, u32[]{:S(2)}, u32[]{:S(2)}) %collective-permute-start.10) | collective-permute-done | bytes 331808 | tf_op jit(solution)/shard_map/ppermute | solution.py:25
  348.9 11.4 %broadcast_select_fusion.1 = (f32[24,12,48,6]{3,2,0,1:T(8,128)}, f32[24,12,48,6]{3,2,0,1:T(8,128)}) fusion(f32[24,12,48,6]{3,2,0,1:T(8,128)} %copy.45, f32[24,12,48,6]{3,2,0,1:T(8,128)} %copy.46, pred[]{:T(512)S(6)} %eq.42), kind=kLoop, calls=%fused_computation.266 | loop fusion | flops 165888 | bytes 1327105 | tf_op jit(solution)/shard_map/jit(_where)/select_n | solution.py:40
  360.3 34.9 %collective-permute-done.6 = f32[24,6,48,48]{3,2,0,1:T(8,128)} collective-permute-done((f32[24,6,48,48]{3,2,0,1:T(8,128)}, f32[24,6,48,48]{3,2,0,1:T(8,128)}, u32[]{:S(2)}, u32[]{:S(2)}) %collective-permute-start.6) | collective-permute-done | bytes 1327136 | tf_op jit(solution)/shard_map/ppermute | solution.py:25
  395.2 5.5 broadcast_select_fusion.5
  400.8 141.7 %fusion.11 = f32[24,12,48,48]{3,2,0,1:T(8,128)} fusion(f32[24,12,48,48]{3,2,0,1:T(8,128)} %reshape.19, f32[24,12,48,48]{3,2,0,1:T(8,128)} %get-tuple-element.5, f32[24,12,6,48]{3,2,0,1:T(8,128)} %get-tuple-element.28, f32[24,12,6,48]{3,2,0,1:T(8,128)} %get-tuple-element.27, f32[24,6,48,48]{3,2,0,1:T(8,128)} %get-tuple-element.14, ...), kind=kLoop, calls=%fused_computation.91 | loop fusion | flops 57065472 | bytes 14708736 | tf_op jit(solution)/shard_map/sub | solution.py:72
  542.5 6.8 copy.49
  549.3 8.8 reshape.20
  558.2 71.9 %all-gather.2.cloned.1.call-done = f32[48,27648]{1,0:T(8,128)} async-done(((f32[24,27648]{1,0:T(8,128)}), f32[48,27648]{1,0:T(8,128)}) %all-gather.2.cloned.1.call-update) | async-done | bytes 5308432 | tf_op jit(solution)/shard_map/all_gather | solution.py:77
  630.1 8.4 fusion.152
  638.5 329.6 %psum.7 = f32[48,48]{0,1:T(8,128)S(1)} all-reduce(f32[48,48]{0,1:T(8,128)S(1)} %fusion.152), channel_id=1, replica_groups=mesh['band'=2,'dom'=64] {'dom'}, use_global_device_ids=true, to_apply=%region_0.1 | all-reduce | flops 2304 | bytes 18432 | tf_op jit(solution)/shard_map/psum | solution.py:79
  (53 shorter events, 79.4 us)
Async XLA Ops:
  6.5 623.6 %all-gather.2.cloned.1.call-start = ((), (), s32[]{:S(2)}) async-start(), calls=%async_computation | async-start | bytes 7962624 | tf_op jit(solution)/shard_map/all_gather | solution.py:77
  17.6 70.4 %collective-permute-start.3 = (f32[24,12,6,48]{3,0,2,1:T(8,128)}, f32[24,12,6,48]{3,0,2,1:T(8,128)}, u32[]{:S(2)}, u32[]{:S(2)}) collective-permute-start(f32[24,12,6,48]{3,0,2,1:T(8,128)} %copy.26), channel_id=1, source_target_pairs={{0,4},{1,5},{2,6},{3,7},{4,0},{5,1},{6,2},{7,3},{8,12},{9,13},{10,... | collective-permute-start | bytes 995336 | tf_op jit(solution)/shard_map/ppermute | solution.py:25
  22.6 65.4 %collective-permute-start.2 = (f32[24,12,6,48]{3,0,2,1:T(8,128)}, f32[24,12,6,48]{3,0,2,1:T(8,128)}, u32[]{:S(2)}, u32[]{:S(2)}) collective-permute-start(f32[24,12,6,48]{3,0,2,1:T(8,128)} %copy.25), channel_id=1, source_target_pairs={{0,8},{1,9},{2,10},{3,11},{4,12},{5,13},{6,14},{7,15},{8,0},{9,1},... | collective-permute-start | bytes 995336 | tf_op jit(solution)/shard_map/ppermute | solution.py:25
  42.1 40.5 %collective-permute-start.5 = (f32[24,12,48,6]{2,0,3,1:T(8,128)}, f32[24,12,48,6]{2,0,3,1:T(8,128)}, u32[]{:S(2)}, u32[]{:S(2)}) collective-permute-start(f32[24,12,48,6]{2,0,3,1:T(8,128)} %copy.32), channel_id=1, source_target_pairs={{0,16},{1,17},{2,18},{3,19},{4,20},{5,21},{6,22},{7,23},{8,24},{9,... | collective-permute-start | bytes 995336 | tf_op jit(solution)/shard_map/ppermute | solution.py:25
  50.8 22.4 %collective-permute-start.4 = (f32[24,12,48,6]{2,0,3,1:T(8,128)}, f32[24,12,48,6]{2,0,3,1:T(8,128)}, u32[]{:S(2)}, u32[]{:S(2)}) collective-permute-start(f32[24,12,48,6]{2,0,3,1:T(8,128)} %copy.31), channel_id=1, source_target_pairs={{0,32},{1,33},{2,34},{3,35},{4,36},{5,37},{6,38},{7,39},{8,40},{9,... | collective-permute-start | bytes 995336 | tf_op jit(solution)/shard_map/ppermute | solution.py:25
  58.3 77.5 %collective-permute-start = (f32[24,6,48,48]{3,2,0,1:T(8,128)}, f32[24,6,48,48]{3,2,0,1:T(8,128)}, u32[]{:S(2)}, u32[]{:S(2)}) collective-permute-start(f32[24,6,48,48]{3,2,0,1:T(8,128)} %get-tuple-element.21), channel_id=1, source_target_pairs={{0,2},{1,3},{2,0},{3,1},{4,6},{5,7},{6,4},{7,5},{8,10},{9,11},{10,... | collective-permute-start | bytes 3981320 | tf_op jit(solution)/shard_map/ppermute | solution.py:25
  73.1 62.7 %collective-permute-start.1 = (f32[24,6,48,48]{3,2,0,1:T(8,128)S(1)}, f32[24,6,48,48]{3,2,0,1:T(8,128)}, u32[]{:S(2)}, u32[]{:S(2)}) collective-permute-start(f32[24,6,48,48]{3,2,0,1:T(8,128)S(1)} %get-tuple-element.22), channel_id=1, source_target_pairs={{0,1},{1,0},{2,3},{3,2},{4,5},{5,4},{6,7},{7,6},{8,9},{9,8},{10,11... | collective-permute-start | bytes 3981320 | tf_op jit(solution)/shard_map/ppermute | solution.py:25
  298.9 46.8 %collective-permute-start.9 = (f32[24,12,6,48]{3,0,2,1:T(8,128)}, f32[24,12,6,48]{3,0,2,1:T(8,128)}, u32[]{:S(2)}, u32[]{:S(2)}) collective-permute-start(f32[24,12,6,48]{3,0,2,1:T(8,128)} %copy.38), channel_id=1, source_target_pairs={{0,4},{1,5},{2,6},{3,7},{4,0},{5,1},{6,2},{7,3},{8,12},{9,13},{10,... | collective-permute-start | bytes 995336 | tf_op jit(solution)/shard_map/ppermute | solution.py:25
  299.3 46.3 %collective-permute-start.8 = (f32[24,12,6,48]{3,0,2,1:T(8,128)}, f32[24,12,6,48]{3,0,2,1:T(8,128)}, u32[]{:S(2)}, u32[]{:S(2)}) collective-permute-start(f32[24,12,6,48]{3,0,2,1:T(8,128)} %copy.37), channel_id=1, source_target_pairs={{0,8},{1,9},{2,10},{3,11},{4,12},{5,13},{6,14},{7,15},{8,0},{9,1},... | collective-permute-start | bytes 995336 | tf_op jit(solution)/shard_map/ppermute | solution.py:25
  311.0 23.0 %copy-start = (f32[12,48,48]{2,1,0:T(8,128)S(1)}, f32[12,48,48]{2,1,0:T(8,128)}, u32[]{:S(2)}) copy-start(f32[12,48,48]{2,1,0:T(8,128)} %mul.99) | copy-start | bytes 331780
  311.0 29.2 %collective-permute-start.11 = (f32[24,12,48,6]{2,0,3,1:T(8,128)}, f32[24,12,48,6]{2,0,3,1:T(8,128)}, u32[]{:S(2)}, u32[]{:S(2)}) collective-permute-start(f32[24,12,48,6]{2,0,3,1:T(8,128)} %copy.44), channel_id=1, source_target_pairs={{0,16},{1,17},{2,18},{3,19},{4,20},{5,21},{6,22},{7,23},{8,24},{9,... | collective-permute-start | bytes 995336 | tf_op jit(solution)/shard_map/ppermute | solution.py:25
  312.6 20.5 %collective-permute-start.10 = (f32[24,12,48,6]{2,0,3,1:T(8,128)}, f32[24,12,48,6]{2,0,3,1:T(8,128)S(1)}, u32[]{:S(2)}, u32[]{:S(2)}) collective-permute-start(f32[24,12,48,6]{2,0,3,1:T(8,128)} %copy.43), channel_id=1, source_target_pairs={{0,32},{1,33},{2,34},{3,35},{4,36},{5,37},{6,38},{7,39},{8,40},{9,... | collective-permute-start | bytes 995336 | tf_op jit(solution)/shard_map/ppermute | solution.py:25
  319.5 75.7 %collective-permute-start.6 = (f32[24,6,48,48]{3,2,0,1:T(8,128)}, f32[24,6,48,48]{3,2,0,1:T(8,128)}, u32[]{:S(2)}, u32[]{:S(2)}) collective-permute-start(f32[24,6,48,48]{3,2,0,1:T(8,128)} %get-tuple-element.15), channel_id=1, source_target_pairs={{0,2},{1,3},{2,0},{3,1},{4,6},{5,7},{6,4},{7,5},{8,10},{9,11},{10,... | collective-permute-start | bytes 3981320 | tf_op jit(solution)/shard_map/ppermute | solution.py:25
  333.1 1.0 copy-start.1
  333.1 62.1 %collective-permute-start.7 = (f32[24,6,48,48]{3,2,0,1:T(8,128)S(1)}, f32[24,6,48,48]{3,2,0,1:T(8,128)}, u32[]{:S(2)}, u32[]{:S(2)}) collective-permute-start(f32[24,6,48,48]{3,2,0,1:T(8,128)S(1)} %get-tuple-element.16), channel_id=1, source_target_pairs={{0,1},{1,0},{2,3},{3,2},{4,5},{5,4},{6,7},{7,6},{8,9},{9,8},{10,11... | collective-permute-start | bytes 3981320 | tf_op jit(solution)/shard_map/ppermute | solution.py:25
Sparse Core Ops, SparseCore 0:
  558.3 71.7 all-gather.1
where the time goes:
time: 1000 us; the launch traced here: 994 us
  other arithmetic  374 us (37%)
  blocking collectives  330 us (33%)
  waiting for transfers between devices  166 us (17%)
  local copies, waits for them, and re-layouts  80.3 us (8%)
  starting transfers between devices  16.8 us (2%)
  between operations  13.7 us (1%)
  matrix products  13.2 us (1%)
    psum x1, blocking collectives, body(): gram = lax.psum(gram, 'dom') * scale  330 us
    sub x1, other arithmetic, body(): 2.0 * (apply_h(first, pot) - centre_shift * first) / half_width - field  142 us
    div x1, other arithmetic, body(): first = (apply_h(field, pot) - centre_shift * field) / half_width  141 us
    ppermute x12, waiting for transfers between devices, swapped(): lax.ppermute(value, axis, [(i, i ^ 1 << apart) for i in range(lax.axis_si...  94.3 us
    all_gather x1, waiting for transfers between devices, body(): every = lax.all_gather(own_flat, 'band', axis=0, tiled=True)  71.9 us
    select_n x6, other arithmetic, padded_along(): upper_rim = jnp.where(odd, received[1], received[0])  40.4 us
    select_n x6, other arithmetic, padded_along(): outgoing = jnp.where(odd == (bit == 1), high_face, low_face)  39.1 us
    select_n x8, local copies, waits for them, and re-layouts, padded_along(): outgoing = jnp.where(odd == (bit == 1), high_face, low_face)  27.5 us
  transfers between devices with their start and end apart: 13, of which 5 were waited for; matrix products, arithmetic and copies ran while one was open for 10% of the time, Pallas kernels for 0%

commit v1 on v0

v1 whole, which is shorter than its diff:
```python
import functools

import jax
import jax.numpy as jnp
import numpy as np
from jax import lax
from jax.experimental import pallas as pl
from jax.experimental.pallas import tpu as pltpu
from jax.sharding import PartitionSpec as P

CX = 12
CY = 48
CZ = 48
CYZ = CY * CZ
LANES = 3 * 128 + CYZ + 3 * 128
MESH = pl.DeviceIdType.MESH
BF = jnp.bfloat16
F32 = jnp.float32

stencil_weights = (
    -5369.0 / 1800.0,
    12.0 / 7.0,
    -15.0 / 56.0,
    10.0 / 189.0,
    -1.0 / 112.0,
    2.0 / 1925.0,
    -1.0 / 16632.0,
)
centre_shift = 7.25
half_width = 5.25
near = [-0.5 * w / half_width for w in stencil_weights]
own = (-1.5 * stencil_weights[0] - centre_shift) / half_width


def split_np(a):
    a = a.astype(np.float32)
    high = a.astype(BF)
    return high, (a - high.astype(np.float32)).astype(BF)


def yz_weights():
    out = np.zeros((3, 1280, 256), np.float64)
    for part in range(3):
        for n in range(256):
            cell = 256 * part + n
            row, z = cell // CZ, cell % CZ
            for k in range(1, 7):
                for sign in (-1, 1):
                    out[part, n + 384 + sign * CZ * k, n] += near[k]
                    at = z + sign * k
                    if 0 <= at < CZ:
                        out[part, n + 384 + sign * k, n] += near[k]
                    elif at < 0:
                        out[part, 1024 + row * 6 + at + 6, n] += near[k]
                    else:
                        out[part, 1152 + row * 6 + at - CZ, n] += near[k]
    return split_np(out)


def face_weights():
    out = np.zeros((768, 256), np.float32)
    for row in range(16):
        for i in range(6):
            out[row * CZ + i, row * 6 + i] = 1
            out[row * CZ + CZ - 6 + i, 128 + row * 6 + i] = 1
    return out.astype(BF)


def split(v):
    high = v.astype(BF)
    return high, (v - high.astype(F32)).astype(BF)


def dot(a, b):
    return jnp.dot(a, b, preferred_element_type=F32)


def dot_t(a, b):
    return lax.dot_general(a, b, (((1,), (1,)), ((), ())), preferred_element_type=F32)


def flipped(index, bit):
    return index + bit * (1 - 2 * (index // bit % 2))


def filter_kernel(
    orb, pot_hbm, wh_hbm, wl_hbm, sel_hbm, f_hbm, fo_hbm, gram,
    lin, pot, wh, wl, sel, cen, xlo, xhi, zlo, zhi, zlo_out, zhi_out, vh, vl, zh, zl, yz, fil, oth, part, got,
    in_sem, out_sem, send_sem, recv_sem, band_send, band_recv, sum_send, sum_recv,
):
    band, dom = lax.axis_index("band"), lax.axis_index("dom")
    loads = [
        pltpu.make_async_copy(a, b, in_sem.at[i])
        for i, (a, b) in enumerate(((orb, lin), (pot_hbm, pot), (wh_hbm, wh), (wl_hbm, wl), (sel_hbm, sel)))
    ]
    for load in loads:
        load.start()

    partners = [(band, flipped(dom, 1 << bit)) for bit in range(6)] + [(1 - band, dom)]
    barrier = pltpu.get_barrier_semaphore()
    for partner in partners:
        pl.semaphore_signal(barrier, 1, device_id=partner, device_id_type=MESH)

    ends = []
    for first in (1, 4, 16):
        odd = (dom // first % 4 + 1) // 2 % 2
        below = odd * flipped(dom, first) + (1 - odd) * flipped(dom, 2 * first)
        above = odd * flipped(dom, 2 * first) + (1 - odd) * flipped(dom, first)
        ends.append(((band, below), (band, above)))

    def copies(slot):
        middle = pl.ds(384, CYZ)
        table = (
            (cen.at[slot, pl.ds(0, 6), :, middle], xhi.at[slot], ends[0][0]),
            (cen.at[slot, pl.ds(6, 6), :, middle], xlo.at[slot], ends[0][1]),
            (cen.at[slot, :, :, pl.ds(384, 384)], cen.at[slot, :, :, pl.ds(384 + CYZ, 384)], ends[1][0]),
            (cen.at[slot, :, :, pl.ds(CYZ, 384)], cen.at[slot, :, :, pl.ds(0, 384)], ends[1][1]),
            (zlo_out.at[slot], zhi.at[slot], ends[2][0]),
            (zhi_out.at[slot], zlo.at[slot], ends[2][1]),
        )
        return [
            pltpu.make_async_remote_copy(a, b, send_sem.at[slot, i], recv_sem.at[slot, i], device_id=to, device_id_type=MESH)
            for i, (a, b, to) in enumerate(table)
        ]

    def band_copy(chunk, half):
        layers = pl.ds(6 * half, 6)
        return pltpu.make_async_remote_copy(
            fil.at[chunk, layers], oth.at[chunk, layers], band_send.at[chunk, half], band_recv.at[chunk, half],
            device_id=(1 - band, dom), device_id_type=MESH,
        )

    def prepare(slot):
        @pl.loop(0, 6)
        def _(i):
            v = cen[slot, pl.ds(2 * i, 2), :, pl.ds(384, CYZ)].reshape(16, CYZ)
            high, low = split(v)
            vh[slot, pl.ds(16 * i, 16), pl.ds(384, CYZ)] = high
            vl[slot, pl.ds(16 * i, 16), pl.ds(384, CYZ)] = low

        for m in range(3):
            lanes = pl.ds(384 + 768 * m, 768)
            faces = dot(vh[slot, :, lanes], sel[...]) + dot(vl[slot, :, lanes], sel[...])
            zlo_out[slot, :, :, pl.ds(128 * m, 128)] = faces[:, :128].reshape(CX, 8, 128)
            zhi_out[slot, :, :, pl.ds(128 * m, 128)] = faces[:, 128:].reshape(CX, 8, 128)
        for copy in copies(slot):
            copy.start()

    def split_rims(slot):
        for start in (0, 384 + CYZ):
            v = cen[slot, :, :, pl.ds(start, 384)].reshape(96, 384)
            high, low = split(v)
            vh[slot, :, pl.ds(start, 384)] = high
            vl[slot, :, pl.ds(start, 384)] = low
        for m in range(3):
            for rim, at in ((zlo, 0), (zhi, 128)):
                v = rim[slot, :, :, pl.ds(128 * m, 128)].reshape(96, 128)
                high, low = split(v)
                zh[:, pl.ds(256 * m + at, 128)] = high
                zl[:, pl.ds(256 * m + at, 128)] = low

    def yz_product(slot):
        @pl.loop(0, 3)
        def _(j):
            start = pl.multiple_of(256 * j, 256)

            def window(v, z):
                return jnp.concatenate(
                    [
                        jnp.concatenate([v[slot, :, pl.ds(start + 768 * m, 1024)], z[:, pl.ds(256 * m, 256)]], 1)
                        for m in range(3)
                    ],
                    0,
                )

            high, low = window(vh, zh), window(vl, zl)
            total = dot(high, wh[j]) + dot(low, wh[j]) + dot(high, wl[j])
            for m in range(3):
                yz[:, pl.ds(start + 768 * m, 256)] = total[96 * m : 96 * m + 96]

    def stencil(slot, write):
        @pl.loop(0, CYZ // 128)
        def _(t):
            at = pl.multiple_of(128 * t, 128)
            here, mid = pl.ds(at, 128), pl.ds(at + 384, 128)
            v = [xlo[slot, i, :, here] for i in range(6)]
            v += [cen[slot, i, :, mid] for i in range(CX)]
            v += [xhi[slot, i, :, here] for i in range(6)]
            for x in range(CX):
                diagonal = pot[pl.ds(18 * x + t, 1), :] * (1.0 / half_width) + own
                total = diagonal * v[x + 6] + yz[pl.ds(8 * x, 8), here]
                for k in range(1, 7):
                    total = total + near[k] * (v[x + 6 - k] + v[x + 6 + k])
                write(x, here, mid, total)

    loads[0].wait()

    def relayout(chunk):
        @pl.loop(0, CX)
        def _(x):
            for t in range(18):
                cen[chunk, x, :, pl.ds(384 + 128 * t, 128)] = lin[pl.ds(8 * 216 * chunk + 18 * x + t, 8, stride=216), :]

    relayout(0)
    loads[4].wait()
    pl.semaphore_wait(barrier, len(partners))

    @pl.loop(0, 3)
    def _(chunk):
        @pl.when(chunk > 0)
        def _():
            relayout(chunk)

        @pl.when(chunk < 2)
        def _():
            prepare(chunk)

    loads[1].wait()
    loads[2].wait()
    loads[3].wait()

    @pl.loop(0, 6)
    def _(step):
        slot = jnp.where(step == 2, 3, jnp.where(step == 3, 2, step))
        for copy in copies(slot):
            copy.wait_recv()
        split_rims(slot)
        yz_product(slot)

        @pl.when(slot < 3)
        def _():
            def write(x, here, mid, total):
                cen[slot + 3, x, :, mid] = total

            stencil(slot, write)
            prepare(slot + 3)

            @pl.when(slot == 0)
            def _():
                prepare(2)

        @pl.when(slot >= 3)
        def _():
            def write(x, here, mid, total):
                fil[slot - 3, x, :, here] = 2.0 * total - cen[slot - 3, x, :, mid]

            stencil(slot, write)
            band_copy(slot - 3, 1 - band).start()
            band_copy(slot - 3, band).start()
            pltpu.make_async_copy(fil.at[slot - 3], f_hbm.at[slot - 3], out_sem.at[slot - 3]).start()

    def rows(ref, x):
        v = ref[:, x].reshape(24, CYZ)
        high, low = split(v)
        return jnp.concatenate([high, low], 0)

    def folded(products):
        return products[:24, :24] + products[24:, :24] + products[:24, 24:]

    part[...] = jnp.zeros_like(part)

    @pl.loop(0, CX)
    def _(x):
        a = rows(fil, x)
        part[0, :, 0:24] += folded(dot_t(a, a))

    for chunk in range(3):
        band_copy(chunk, band).wait_recv()

    @pl.loop(0, 6)
    def _(i):
        x = 6 * band + i
        part[0, :, 24:48] += folded(dot_t(rows(fil, x), rows(oth, x)))

    for bit in range(7):
        copy = pltpu.make_async_remote_copy(
            part.at[bit], got.at[bit], sum_send.at[bit], sum_recv.at[bit], device_id=partners[bit], device_id_type=MESH
        )
        copy.start()
        copy.wait()
        if bit < 6:
            part[bit + 1] = part[bit] + got[bit]

    gram[0] = part[6]
    gram[1] = got[6]
    for chunk in range(3):
        band_copy(chunk, 1 - band).wait_recv()
        pltpu.make_async_copy(oth.at[chunk], fo_hbm.at[chunk], out_sem.at[3 + chunk]).start()
    for chunk in range(3):
        for half in range(2):
            band_copy(chunk, half).wait_send()
        pltpu.make_async_copy(fil.at[chunk], f_hbm.at[chunk], out_sem.at[chunk]).wait()
        pltpu.make_async_copy(oth.at[chunk], fo_hbm.at[chunk], out_sem.at[3 + chunk]).wait()

    @pl.loop(0, 6)
    def _(slot):
        for copy in copies(slot):
            copy.wait_send()


def filter_call(lines, pot):
    wh, wl = yz_weights()
    sel = face_weights()
    any_space = pl.BlockSpec(memory_space=pl.ANY)
    chunk = (3, CX, 8, CYZ)
    vm = pltpu.VMEM
    return pl.pallas_call(
        filter_kernel,
        out_shape=(
            jax.ShapeDtypeStruct(chunk, F32),
            jax.ShapeDtypeStruct(chunk, F32),
            jax.ShapeDtypeStruct((2, 24, 128), F32),
        ),
        in_specs=[any_space] * 5,
        out_specs=(any_space, any_space, pl.BlockSpec(memory_space=pltpu.VMEM)),
        scratch_shapes=[
            vm((24 * 216, 128), F32),
            vm((216, 128), F32),
            vm(wh.shape, BF),
            vm(wl.shape, BF),
            vm(sel.shape, BF),
            vm((6, CX, 8, LANES), F32),
            vm((6, 6, 8, CYZ), F32),
            vm((6, 6, 8, CYZ), F32),
            vm((6, CX, 8, 384), F32),
            vm((6, CX, 8, 384), F32),
            vm((6, CX, 8, 384), F32),
            vm((6, CX, 8, 384), F32),
            vm((6, 96, LANES), BF),
            vm((6, 96, LANES), BF),
            vm((96, 768), BF),
            vm((96, 768), BF),
            vm((96, CYZ), F32),
            vm(chunk, F32),
            vm(chunk, F32),
            vm((7, 24, 128), F32),
            vm((7, 24, 128), F32),
            pltpu.SemaphoreType.DMA((5,)),
            pltpu.SemaphoreType.DMA((6,)),
            pltpu.SemaphoreType.DMA((6, 6)),
            pltpu.SemaphoreType.DMA((6, 6)),
            pltpu.SemaphoreType.DMA((3, 2)),
            pltpu.SemaphoreType.DMA((3, 2)),
            pltpu.SemaphoreType.DMA((7,)),
            pltpu.SemaphoreType.DMA((7,)),
        ],
        compiler_params=pltpu.CompilerParams(collective_id=0, has_side_effects=True, vmem_limit_bytes=56 << 20),
        name="filter",
    )(lines, pot, jnp.asarray(wh), jnp.asarray(wl), jnp.asarray(sel))


def rotate_kernel(low, high, mat, out, mine, theirs, lines, sems, out_sem):
    loads = []
    for x in range(CX):
        loads.append(
            (
                pltpu.make_async_copy(low.at[:, x], mine.at[:, x], sems.at[0, x]),
                pltpu.make_async_copy(high.at[:, x], theirs.at[:, x], sems.at[1, x]),
            )
        )
        for load in loads[-1]:
            load.start()
    mh, ml = split(mat[...])
    left = jnp.concatenate([mh, ml, mh], 1)
    for x in range(CX):
        for load in loads[x]:
            load.wait()
        v = jnp.concatenate([mine[:, x].reshape(24, CYZ), theirs[:, x].reshape(24, CYZ)], 0)
        vh, vl = split(v)
        made = dot(left, jnp.concatenate([vh, vh, vl], 0))
        for t in range(18):
            lines[pl.ds(18 * x + t, 24, stride=216), :] = made[:, 128 * t : 128 * t + 128]
    copy = pltpu.make_async_copy(lines, out, out_sem)
    copy.start()
    copy.wait()


def rotate_call(mine, theirs, mat):
    any_space = pl.BlockSpec(memory_space=pl.ANY)
    vm = pltpu.VMEM
    return pl.pallas_call(
        rotate_kernel,
        out_shape=jax.ShapeDtypeStruct((24 * 216, 128), F32),
        in_specs=[any_space, any_space, pl.BlockSpec(memory_space=pltpu.VMEM)],
        out_specs=any_space,
        scratch_shapes=[
            vm((3, CX, 8, CYZ), F32),
            vm((3, CX, 8, CYZ), F32),
            vm((24 * 216, 128), F32),
            pltpu.SemaphoreType.DMA((2, CX)),
            pltpu.SemaphoreType.DMA,
        ],
        compiler_params=pltpu.CompilerParams(vmem_limit_bytes=56 << 20),
        name="rotate",
    )(mine, theirs, mat)


def body(orbitals, potential):
    group = orbitals.shape[0]
    band = lax.axis_index("band")
    scale = 1.0 / (CX * CYZ * lax.axis_size("dom"))
    mine, theirs, gram = filter_call(orbitals.reshape(group * 216, 128), potential.reshape(216, 128))
    low, high = jnp.where(band == 0, gram, gram[::-1]) * scale
    cross = low[:, 24:48].T + high[:, 24:48]
    whole = jnp.block([[low[:, :24], cross.T], [cross, high[:, :24]]])
    lower = jnp.linalg.cholesky(whole)
    inverse = lax.linalg.triangular_solve(lower, jnp.eye(2 * group, dtype=F32), left_side=True, lower=True)
    rows = lax.dynamic_slice_in_dim(inverse, band * group, group, 0)
    rows = jnp.where(band == 0, rows, jnp.roll(rows, group, 1))
    return rotate_call(mine, theirs, rows).reshape(orbitals.shape)


def solution(mesh):
    return jax.shard_map(
        body,
        mesh=mesh,
        in_specs=(P("band", "dom", None, None), P("dom", None, None)),
        out_specs=P("band", "dom", None, None),
        check_vma=False,
    )
```

time: 1000 us -> 151 us (0.15)
  other arithmetic: 374 us -> 11.2 us
  blocking collectives: 330 us -> 0 us
  waiting for transfers between devices: 166 us -> 0 us
  Pallas kernels: 0 us -> 139 us
  local copies, waits for them, and re-layouts: 80.3 us -> 0.34 us
  starting transfers between devices: 16.8 us -> 0 us
  between operations: 13.7 us -> 0.04 us
  matrix products: 13.2 us -> 0.22 us
    psum x1 -> x0, blocking collectives: 330 us -> none  [body(): gram = lax.psum(gram, 'dom') * scale]
    sub x1 -> x0, other arithmetic: 142 us -> none  [body(): 2.0 * (apply_h(first, pot) - centre_shift * first) / half_width - field]
    div x2 -> x1, other arithmetic: 141 us -> 0.09 us  [body(): lower = jnp.linalg.cholesky(whole)]
    pallas_call x0 -> x2, Pallas kernels: none -> 139 us  [the longest x1 133 us: filter_call(): pl.pallas_call(filter_kernel, out_shape=(jax.ShapeDtypeStruct(chunk, F32)...]
    ppermute x12 -> x0, waiting for transfers between devices: 94.3 us -> none  [swapped(): lax.ppermute(value, axis, [(i, i ^ 1 << apart) for i in range(lax.axis_si...]
    select_n x12 -> x1, other arithmetic: 79.4 us -> 0.68 us  [body(): rows = jnp.where(band == 0, rows, jnp.roll(rows, group, 1))]
    all_gather x1 -> x0, waiting for transfers between devices: 71.9 us -> none  [body(): every = lax.all_gather(own_flat, 'band', axis=0, tiled=True)]
    select_n x8 -> x0, local copies, waits for them, and re-layouts: 27.5 us -> none  [padded_along(): outgoing = jnp.where(odd == (bit == 1), high_face, low_face)]
  transfers between devices with their start and end apart: 13 -> 0, of which waited for: 5 -> 0; matrix products, arithmetic and copies ran while one was open for 10% -> 0% of each run, Pallas kernels for 0% -> 0%
where the time goes in v1:
time: 151 us
  Pallas kernels  139 us (92%)
  other arithmetic  11.2 us (7%)
    pallas_call x1, Pallas kernels, filter_call(): pl.pallas_call(filter_kernel, out_shape=(jax.ShapeDtypeStruct(chunk, F32)...  133 us
    pallas_call x1, Pallas kernels, rotate_call(): pl.pallas_call(rotate_kernel, out_shape=jax.ShapeDtypeStruct((24 * 216, 1...  6.34 us
    another operation x3, other arithmetic, body(): lower = jnp.linalg.cholesky(whole)  5.06 us
    another operation x2, other arithmetic, body(): lax.linalg.triangular_solve(lower, jnp.eye(2 * group, dtype=F32), left_si...  4.32 us

profile of v1, /device:TPU:2, one launch (start us, length us, event | category | flops | bytes accessed | tf_op | source)
XLA Modules:
  0.0 151.2 jit_solution(16659906355235968157)
XLA Ops:
  0.0 133.1 %filter.1 = (f32[3,12,8,2304]{3,2,1,0:T(8,128)}, f32[3,12,8,2304]{3,2,1,0:T(8,128)}, f32[2,24,128]{2,1,0:T(8,128)}) custom-call(f32[5184,128]{1,0:T(8,128)} %bitcast.21, f32[216,128]{1,0:T(8,128)} %bitcast.25, bf16[3,1280,256]{2,1,0:T(8,128)(2,1)} %constant.61.clone.wh_hbm, bf16[3,1280,256]{2,1,0:T(8,128)(2,1)} %constant.62.clone.wl_hbm, ...), custom_call_target="tpu_custom_call" | custom-call | tf_op jit(solution)/shard_map/filter/pallas_call | solution.py:307
  133.1 0.8 fusion.1
  133.9 0.1 copy.10
  134.0 0.1 slice_add_fusion
  134.1 0.1 pad_maximum_fusion
  134.2 0.1 copy.11
  134.3 0.1 maximum_maximum_fusion
  134.3 0.1 copy.12
  134.4 0.1 fusion.4
  134.5 4.4 %cholesky.17 = f32[48,48]{1,0:T(8,128)S(1)} custom-call(f32[48,48]{1,0:T(8,128)S(1)} %fusion.4), custom_call_target="Cholesky" | custom-call | tf_op jit(solution)/shard_map/jit(cholesky)/cholesky | solution.py:406
  138.9 0.6 compare_reduce_fusion
  139.6 0.7 fusion
  140.2 3.7 %custom-call.6 = f32[1,48,48]{1,2,0:T(8,128)S(1)} custom-call(f32[1,48,48]{2,1,0:T(8,128)S(1)} %fusion), custom_call_target="InvertDiagBlocksLowerTriangular" | custom-call | tf_op jit(solution)/shard_map/triangular_solve | solution.py:407
  143.9 0.2 fusion.2
  144.1 0.1 fusion.5
  144.2 0.7 maximum_select_fusion.mat
  144.9 6.3 %rotate.1 = f32[5184,128]{1,0:T(8,128)} custom-call(f32[3,12,8,2304]{3,2,1,0:T(8,128)} %get-tuple-element.8.low, f32[3,12,8,2304]{3,2,1,0:T(8,128)} %get-tuple-element.9.high, f32[24,48]{1,0:T(8,128)} %maximum_select_fusion.mat), custom_call_target="tpu_custom_call" | custom-call | tf_op jit(solution)/shard_map/rotate/pallas_call | solution.py:381
  (2 shorter events, 0.0 us)

commit v2 on v1

v2 whole, which is shorter than its diff:
```python
import jax
import jax.numpy as jnp
import numpy as np
from jax import lax
from jax.experimental import pallas as pl
from jax.experimental.pallas import tpu as pltpu
from jax.sharding import PartitionSpec as P

CX = 12
CY = 48
CZ = 48
CYZ = CY * CZ
LANES = 3 * 128 + CYZ + 3 * 128
MESH = pl.DeviceIdType.MESH
BF = jnp.bfloat16
F32 = jnp.float32

stencil_weights = (
    -5369.0 / 1800.0,
    12.0 / 7.0,
    -15.0 / 56.0,
    10.0 / 189.0,
    -1.0 / 112.0,
    2.0 / 1925.0,
    -1.0 / 16632.0,
)
centre_shift = 7.25
half_width = 5.25
near = [-0.5 * w / half_width for w in stencil_weights]
own = (-1.5 * stencil_weights[0] - centre_shift) / half_width


def split_np(a):
    a = a.astype(np.float32)
    high = a.astype(BF)
    return high, (a - high.astype(np.float32)).astype(BF)


def yz_weights():
    out = np.zeros((3, 1280, 256), np.float64)
    for part in range(3):
        for n in range(256):
            cell = 256 * part + n
            row, z = cell // CZ, cell % CZ
            for k in range(1, 7):
                for sign in (-1, 1):
                    out[part, n + 384 + sign * CZ * k, n] += near[k]
                    at = z + sign * k
                    if 0 <= at < CZ:
                        out[part, n + 384 + sign * k, n] += near[k]
                    elif at < 0:
                        out[part, 1024 + row * 6 + at + 6, n] += near[k]
                    else:
                        out[part, 1152 + row * 6 + at - CZ, n] += near[k]
    return split_np(out)


def face_weights():
    out = np.zeros((768, 256), np.float32)
    for row in range(16):
        for i in range(6):
            out[row * CZ + i, row * 6 + i] = 1
            out[row * CZ + CZ - 6 + i, 128 + row * 6 + i] = 1
    return out.astype(BF)


def split(v):
    high = v.astype(BF)
    return high, (v - high.astype(F32)).astype(BF)


def dot(a, b):
    return jnp.dot(a, b, preferred_element_type=F32)


def dot_t(a, b):
    return lax.dot_general(a, b, (((1,), (1,)), ((), ())), preferred_element_type=F32)


def flipped(index, bit):
    return index + bit * (1 - 2 * (index // bit % 2))


def filter_kernel(
    orb, pot_hbm, wh_hbm, wl_hbm, sel_hbm, f_hbm, fo_hbm, gram,
    lin, pot, wh, wl, sel, cen, xlo, xhi, zlo, zhi, zlo_out, zhi_out, vh, vl, yz, fil, oth, part, got,
    in_sem, out_sem, send_sem, recv_sem, band_send, band_recv, sum_send, sum_recv,
):
    band, dom = lax.axis_index("band"), lax.axis_index("dom")
    loads = [
        pltpu.make_async_copy(a, b, in_sem.at[i])
        for i, (a, b) in enumerate(((orb, lin), (pot_hbm, pot), (wh_hbm, wh), (wl_hbm, wl), (sel_hbm, sel)))
    ]
    for load in loads:
        load.start()

    def across(z, core, y, x, other):
        to = dom
        for bit, used in enumerate((core, z % 2, z // 2, y % 2, y // 2, x)):
            if used:
                to = flipped(to, 1 << bit)
        return (1 - band if other else band), to

    stages = [
        [across(0, 0, 0, k % 2, k // 2) for k in range(1, 4)],
        [across(k // 2, k % 2, 0, 0, 0) for k in range(1, 8)],
        [across(0, 0, k, 0, 0) for k in range(1, 4)],
    ]
    partners = [partner for stage in stages for partner in stage]
    barrier = pltpu.get_barrier_semaphore()
    for partner in partners:
        pl.semaphore_signal(barrier, 1, device_id=partner, device_id_type=MESH)

    ends = []
    for first in (1, 4, 16):
        odd = (dom // first % 4 + 1) // 2 % 2
        below = odd * flipped(dom, first) + (1 - odd) * flipped(dom, 2 * first)
        above = odd * flipped(dom, 2 * first) + (1 - odd) * flipped(dom, first)
        ends.append(((band, below), (band, above)))

    def copies(slot, m):
        lanes, centre, face = pl.ds(768 * m, 768), pl.ds(384 + 768 * m, 768), pl.ds(128 * m, 128)
        table = (
            (cen.at[slot, pl.ds(0, 6), :, centre], xhi.at[slot, :, :, lanes], ends[0][0]),
            (cen.at[slot, pl.ds(6, 6), :, centre], xlo.at[slot, :, :, lanes], ends[0][1]),
            (zlo_out.at[slot, :, :, face], zhi.at[slot, :, :, face], ends[2][0]),
            (zhi_out.at[slot, :, :, face], zlo.at[slot, :, :, face], ends[2][1]),
        )
        return [
            pltpu.make_async_remote_copy(
                a, b, send_sem.at[slot, m, i], recv_sem.at[slot, m, i], device_id=to, device_id_type=MESH
            )
            for i, (a, b, to) in enumerate(table)
        ]

    def low_copy(slot):
        return pltpu.make_async_remote_copy(
            cen.at[slot, :, :, pl.ds(384, 384)], cen.at[slot, :, :, pl.ds(384 + CYZ, 384)],
            send_sem.at[slot, 0, 4], recv_sem.at[slot, 0, 4], device_id=ends[1][0], device_id_type=MESH,
        )

    def high_copy(slot):
        return pltpu.make_async_remote_copy(
            cen.at[slot, :, :, pl.ds(CYZ, 384)], cen.at[slot, :, :, pl.ds(0, 384)],
            send_sem.at[slot, 2, 4], recv_sem.at[slot, 2, 4], device_id=ends[1][1], device_id_type=MESH,
        )

    def band_copy(chunk, m, half):
        part_of = (chunk, pl.ds(6 * half, 6), slice(None), pl.ds(768 * m, 768))
        return pltpu.make_async_remote_copy(
            fil.at[part_of], oth.at[part_of], band_send.at[chunk, m, half], band_recv.at[chunk, m, half],
            device_id=(1 - band, dom), device_id_type=MESH,
        )

    def group(i):
        return 2 * i % 3

    def prepare(slot, m):
        lanes = pl.ds(pl.multiple_of(384 + 768 * m, 128), 768)
        face = pl.ds(pl.multiple_of(128 * m, 128), 128)
        high, low = split(cen[slot, :, :, lanes].reshape(96, 768))
        vh[slot, :, lanes] = high
        vl[slot, :, lanes] = low
        faces = dot(high, sel[...]) + dot(low, sel[...])
        zlo_out[slot, :, :, face] = faces[:, :128].reshape(CX, 8, 128)
        zhi_out[slot, :, :, face] = faces[:, 128:].reshape(CX, 8, 128)
        for copy in copies(slot, m):
            copy.start()

        @pl.when(m == 0)
        def _():
            low_copy(slot).start()

        @pl.when(m == 2)
        def _():
            high_copy(slot).start()

    def split_rim(slot, start):
        high, low = split(cen[slot, :, :, pl.ds(start, 384)].reshape(96, 384))
        vh[slot, :, pl.ds(start, 384)] = high
        vl[slot, :, pl.ds(start, 384)] = low

    def receive(slot, m):
        for copy in copies(slot, m):
            copy.wait_recv()

        @pl.when(m == 0)
        def _():
            high_copy(slot).wait_recv()
            split_rim(slot, 0)

        @pl.when(m == 2)
        def _():
            low_copy(slot).wait_recv()
            split_rim(slot, 384 + CYZ)

    def yz_product(slot, m):
        face = pl.ds(pl.multiple_of(128 * m, 128), 128)
        rims = jnp.concatenate([zlo[slot, :, :, face].reshape(96, 128), zhi[slot, :, :, face].reshape(96, 128)], 1)
        zh, zl = split(rims)
        for j in range(3):
            window = pl.ds(pl.multiple_of(256 * j + 768 * m, 256), 1024)
            high = jnp.concatenate([vh[slot, :, window], zh], 1)
            low = jnp.concatenate([vl[slot, :, window], zl], 1)
            yz[:, pl.ds(256 * j, 256)] = dot(high, wh[j]) + dot(low, wh[j]) + dot(high, wl[j])

    def stencil(slot, m, write):
        @pl.loop(0, 6)
        def _(t):
            at = pl.multiple_of(768 * m + 128 * t, 128)
            here, mid = pl.ds(at, 128), pl.ds(pl.multiple_of(at + 384, 128), 128)
            v = [xlo[slot, i, :, here] for i in range(6)]
            v += [cen[slot, i, :, mid] for i in range(CX)]
            v += [xhi[slot, i, :, here] for i in range(6)]
            for x in range(CX):
                diagonal = pot[pl.ds(18 * x + 6 * m + t, 1), :] * (1.0 / half_width) + own
                total = diagonal * v[x + 6] + yz[pl.ds(8 * x, 8), pl.ds(pl.multiple_of(128 * t, 128), 128)]
                for k in range(1, 7):
                    total = total + near[k] * (v[x + 6 - k] + v[x + 6 + k])
                write(x, here, mid, total)

    def relayout(chunk, m):
        for x in range(CX):
            for t in range(6):
                row = 8 * 216 * chunk + 18 * x + 6 * m + t
                lanes = pl.ds(pl.multiple_of(384 + 768 * m + 128 * t, 128), 128)
                cen[chunk, x, :, lanes] = lin[pl.ds(row, 8, stride=216), :]

    def enter(chunk, m):
        relayout(chunk, m)
        prepare(chunk, m)

    loads[0].wait()
    loads[4].wait()
    pl.semaphore_wait(barrier, len(partners))

    @pl.loop(0, 3)
    def _(i):
        enter(0, group(i))

    for load in loads[1:4]:
        load.wait()

    @pl.loop(0, 3)
    def _(chunk):
        @pl.loop(0, 3)
        def _(i):
            m = group(i)
            receive(chunk, m)

            def write(x, here, mid, total):
                cen[chunk + 3, x, :, mid] = total

            yz_product(chunk, m)
            stencil(chunk, m, write)
            prepare(chunk + 3, m)

        @pl.loop(0, 3)
        def _(i):
            m = group(i)
            receive(chunk + 3, m)

            @pl.when(chunk < 2)
            def _():
                enter(chunk + 1, m)

            def write(x, here, mid, total):
                fil[chunk, x, :, here] = 2.0 * total - cen[chunk, x, :, mid]

            yz_product(chunk + 3, m)
            stencil(chunk + 3, m, write)
            band_copy(chunk, m, 1 - band).start()

            @pl.when((band == 0) & (chunk < 2))
            def _():
                band_copy(chunk, m, 0).start()

        pltpu.make_async_copy(fil.at[chunk], f_hbm.at[chunk], out_sem.at[chunk]).start()

    def rows(ref, x):
        v = ref[:, x].reshape(24, CYZ)
        high, low = split(v)
        return jnp.concatenate([high, low], 0)

    def folded(a, b):
        products = dot_t(a, b)
        return products[:24, :24] + products[24:, :24] + products[:24, 24:]

    part[...] = jnp.zeros_like(part)

    @pl.loop(0, CX)
    def _(x):
        a = rows(fil, x)
        part[0, :, 0:24] += folded(a, a)

    part[0] = jnp.where(band == 0, part[0], pltpu.roll(part[0], 32, 1))

    @pl.loop(0, 3)
    def _(chunk):
        for m in range(3):
            band_copy(chunk, m, band).wait_recv()

    @pl.loop(0, 6)
    def _(i):
        mine, theirs = rows(fil, 6 * band + i), rows(oth, 6 * band + i)
        first, second = jnp.where(band == 0, mine, theirs), jnp.where(band == 0, theirs, mine)
        part[0, :, 64:88] += folded(second, first)
        part[0, :, 96:120] += folded(first, second)

    index = 0
    for number, stage in enumerate(stages):
        moves = []
        for partner in stage:
            moves.append(
                pltpu.make_async_remote_copy(
                    part.at[number], got.at[index], sum_send.at[index], sum_recv.at[index],
                    device_id=partner, device_id_type=MESH,
                )
            )
            moves[-1].start()
            index += 1
        for move in moves:
            move.wait_recv()
        if number == 0:

            @pl.when(band == 0)
            def _():
                for m in range(3):
                    band_copy(2, m, 0).start()

        terms = [part[number]] + [got[index - len(stage) + k] for k in range(len(stage))]
        while len(terms) > 1:
            terms = [a + b for a, b in zip(terms[::2], terms[1::2])]
        if number < 2:
            part[number + 1] = terms[0]
        else:
            gram[...] = terms[0]
        for move in moves:
            move.wait_send()

    @pl.when(band == 1)
    def _():
        @pl.loop(0, 3)
        def _(chunk):
            for m in range(3):
                band_copy(chunk, m, 0).wait_recv()
            copy = pltpu.make_async_copy(oth.at[chunk], fo_hbm.at[chunk], out_sem.at[3 + chunk])
            copy.start()
            copy.wait()

    @pl.loop(0, 6)
    def _(slot):
        for m in range(3):
            for copy in copies(slot, m):
                copy.wait_send()
        low_copy(slot).wait_send()
        high_copy(slot).wait_send()

    @pl.loop(0, 3)
    def _(chunk):
        for m in range(3):
            band_copy(chunk, m, 1 - band).wait_send()

            @pl.when(band == 0)
            def _():
                band_copy(chunk, m, 0).wait_send()

        pltpu.make_async_copy(fil.at[chunk], f_hbm.at[chunk], out_sem.at[chunk]).wait()


def filter_call(lines, pot):
    wh, wl = yz_weights()
    sel = face_weights()
    any_space = pl.BlockSpec(memory_space=pl.ANY)
    chunk = (3, CX, 8, CYZ)
    vm = pltpu.VMEM
    return pl.pallas_call(
        filter_kernel,
        out_shape=(
            jax.ShapeDtypeStruct(chunk, F32),
            jax.ShapeDtypeStruct(chunk, F32),
            jax.ShapeDtypeStruct((24, 128), F32),
        ),
        in_specs=[any_space] * 5,
        out_specs=(any_space, any_space, pl.BlockSpec(memory_space=pltpu.VMEM)),
        scratch_shapes=[
            vm((24 * 216, 128), F32),
            vm((216, 128), F32),
            vm(wh.shape, BF),
            vm(wl.shape, BF),
            vm(sel.shape, BF),
            vm((6, CX, 8, LANES), F32),
            vm((6, 6, 8, CYZ), F32),
            vm((6, 6, 8, CYZ), F32),
            vm((6, CX, 8, 384), F32),
            vm((6, CX, 8, 384), F32),
            vm((6, CX, 8, 384), F32),
            vm((6, CX, 8, 384), F32),
            vm((6, 96, LANES), BF),
            vm((6, 96, LANES), BF),
            vm((96, 768), F32),
            vm(chunk, F32),
            vm(chunk, F32),
            vm((3, 24, 128), F32),
            vm((13, 24, 128), F32),
            pltpu.SemaphoreType.DMA((5,)),
            pltpu.SemaphoreType.DMA((6,)),
            pltpu.SemaphoreType.DMA((6, 3, 5)),
            pltpu.SemaphoreType.DMA((6, 3, 5)),
            pltpu.SemaphoreType.DMA((3, 3, 2)),
            pltpu.SemaphoreType.DMA((3, 3, 2)),
            pltpu.SemaphoreType.DMA((13,)),
            pltpu.SemaphoreType.DMA((13,)),
        ],
        compiler_params=pltpu.CompilerParams(collective_id=0, has_side_effects=True, vmem_limit_bytes=56 << 20),
        name="filter",
    )(lines, pot, jnp.asarray(wh), jnp.asarray(wl), jnp.asarray(sel))


def rotate_kernel(low, high, gram, out, mine, theirs, inverse, lines, sems, out_sems):
    band = lax.axis_index("band")

    def loads(x):
        own_load = pltpu.make_async_copy(low.at[:, x], mine.at[:, x], sems.at[0, x])
        return own_load, pltpu.make_async_copy(high.at[:, x], theirs.at[:, x], sems.at[1, x])

    for x in range(CX):
        loads(x)[0].start()

        @pl.when(band == 1)
        def _():
            loads(x)[1].start()

    g = gram[...] * (1.0 / (64 * CX * CYZ))
    blank = jnp.zeros((24, 16), F32)
    row, col = (lax.broadcasted_iota(jnp.int32, (48, 64), d) for d in range(2))
    left = jnp.concatenate(
        [jnp.concatenate([g[:, 0:24], g[:, 96:120], blank], 1), jnp.concatenate([g[:, 64:88], g[:, 32:56], blank], 1)], 0
    )
    table = jnp.concatenate([left, (row == col).astype(F32)], 1)
    rows = lax.broadcasted_iota(jnp.int32, (48, 128), 0)
    for k in range(0, 48, 2):
        one = jnp.broadcast_to(table[:, k : k + 1], (48, 128))
        two = jnp.broadcast_to(table[:, k + 1 : k + 2], (48, 128))
        a, b, c = one[k : k + 1], one[k + 1 : k + 2], two[k + 1 : k + 2]
        upper, lower = table[k : k + 1], table[k + 1 : k + 2]
        inverse[k : k + 1, :] = upper * lax.rsqrt(a)
        ratio = b / a
        inverse[k + 1 : k + 2, :] = (lower - ratio * upper) * lax.rsqrt(c - ratio * b)
        if k < 46:
            scale = 1.0 / (a * c - b * b)
            below = rows > k + 1
            table = (
                table
                - jnp.where(below, one, 0.0) * ((c * upper - b * lower) * scale)
                - jnp.where(below, two, 0.0) * ((a * lower - b * upper) * scale)
            )

    def sent(quarter):
        at = pl.ds(72 * quarter, 72)
        return pltpu.make_async_copy(lines.reshape(24, 216, 128).at[:, at], out.at[:, at], out_sems.at[quarter])

    def rotate(matrix, sources):
        mh, ml = split(matrix)
        left = jnp.concatenate([mh, ml, mh], 1)
        for x in range(CX):
            for load in loads(x)[: len(sources)]:
                load.wait()
            v = [source[:, x].reshape(24, CYZ) for source in sources]
            vh, vl = split(jnp.concatenate(v, 0) if len(v) > 1 else v[0])
            made = dot(left, jnp.concatenate([vh, vh, vl], 0))
            for t in range(18):
                lines[pl.ds(18 * x + t, 24, stride=216), :] = made[:, 128 * t : 128 * t + 128]
            if x % 4 == 3:
                sent(x // 4).start()

    @pl.when(band == 0)
    def _():
        rotate(inverse[0:24, 64:88], [mine])

    @pl.when(band == 1)
    def _():
        rotate(jnp.concatenate([inverse[24:48, 88:112], inverse[24:48, 64:88]], 1), [mine, theirs])

    for quarter in range(3):
        sent(quarter).wait()


def rotate_call(mine, theirs, gram):
    any_space = pl.BlockSpec(memory_space=pl.ANY)
    vm = pltpu.VMEM
    return pl.pallas_call(
        rotate_kernel,
        out_shape=jax.ShapeDtypeStruct((24, 216, 128), F32),
        in_specs=[any_space, any_space, pl.BlockSpec(memory_space=pltpu.VMEM)],
        out_specs=any_space,
        scratch_shapes=[
            vm((3, CX, 8, CYZ), F32),
            vm((3, CX, 8, CYZ), F32),
            vm((48, 128), F32),
            vm((24 * 216, 128), F32),
            pltpu.SemaphoreType.DMA((2, CX)),
            pltpu.SemaphoreType.DMA((3,)),
        ],
        compiler_params=pltpu.CompilerParams(vmem_limit_bytes=56 << 20),
        name="rotate",
    )(mine, theirs, gram)


def body(orbitals, potential):
    mine, theirs, gram = filter_call(orbitals.reshape(24 * 216, 128), potential.reshape(216, 128))
    return rotate_call(mine, theirs, gram).reshape(orbitals.shape)


def solution(mesh):
    return jax.shard_map(
        body,
        mesh=mesh,
        in_specs=(P("band", "dom", None, None), P("dom", None, None)),
        out_specs=P("band", "dom", None, None),
        check_vma=False,
    )
```

time: 151 us -> 121 us (0.80)
  Pallas kernels: 139 us -> 120 us
  other arithmetic: 11.2 us -> 0 us
    pallas_call x1, Pallas kernels: 133 us -> 113 us  [filter_call(): pl.pallas_call(filter_kernel, out_shape=(jax.ShapeDtypeStruct(chunk, F32)...]
    another operation x5 -> x0, other arithmetic: 9.38 us -> none  [the longest x3 5.06 us: body(): lower = jnp.linalg.cholesky(whole)]
where the time goes in v2:
time: 121 us; the launch traced here: 120 us
  Pallas kernels  120 us (99%)
    pallas_call x1, Pallas kernels, filter_call(): pl.pallas_call(filter_kernel, out_shape=(jax.ShapeDtypeStruct(chunk, F32)...  113 us
    pallas_call x1, Pallas kernels, rotate_call(): pl.pallas_call(rotate_kernel, out_shape=jax.ShapeDtypeStruct((24, 216, 12...  7.15 us

profile of v2, /device:TPU:2, one launch (start us, length us, event | category | flops | bytes accessed | tf_op | source)
XLA Modules:
  0.0 120.1 jit_solution(9076280670597190669)
XLA Ops:
  0.0 112.9 %filter.1 = (f32[3,12,8,2304]{3,2,1,0:T(8,128)}, f32[3,12,8,2304]{3,2,1,0:T(8,128)}, f32[24,128]{1,0:T(8,128)}) custom-call(f32[5184,128]{1,0:T(8,128)} %bitcast.3, f32[216,128]{1,0:T(8,128)} %bitcast.4, bf16[3,1280,256]{2,1,0:T(8,128)(2,1)} %constant.6.clone.wh_hbm, bf16[3,1280,256]{2,1,0:T(8,128)(2,1)} %constant.7.clone.wl_hbm, ...), custom_call_target="tpu_custom_call" | custom-call | tf_op jit(solution)/shard_map/filter/pallas_call | solution.py:377
  112.9 7.1 %rotate.1 = f32[24,216,128]{2,1,0:T(8,128)} custom-call(f32[3,12,8,2304]{3,2,1,0:T(8,128)} %get-tuple-element.8.low, f32[3,12,8,2304]{3,2,1,0:T(8,128)} %get-tuple-element.9.high, f32[24,128]{1,0:T(8,128)} %get-tuple-element.10.gram), custom_call_target="tpu_custom_call" | custom-call | tf_op jit(solution)/shard_map/rotate/pallas_call | solution.py:492

commit v3 on v2

--- a/solution.py
+++ b/solution.py
@@ -83,14 +83,13 @@
 
 def filter_kernel(
     orb, pot_hbm, wh_hbm, wl_hbm, sel_hbm, f_hbm, fo_hbm, gram,
-    lin, pot, wh, wl, sel, cen, xlo, xhi, zlo, zhi, zlo_out, zhi_out, vh, vl, yz, fil, oth, part, got,
+    lin, pot, wh, wl, sel, cen, xlo, xhi, zlo, zhi, zlo_out, zhi_out, ylo, yhi, ylo_out, yhi_out, vh, vl, yz, fil, oth, part, got,
     in_sem, out_sem, send_sem, recv_sem, band_send, band_recv, sum_send, sum_recv,
 ):
     band, dom = lax.axis_index("band"), lax.axis_index("dom")
-    loads = [
-        pltpu.make_async_copy(a, b, in_sem.at[i])
-        for i, (a, b) in enumerate(((orb, lin), (pot_hbm, pot), (wh_hbm, wh), (wl_hbm, wl), (sel_hbm, sel)))
-    ]
+    pairs = [(orb.at[pl.ds(1728 * c, 1728)], lin.at[pl.ds(1728 * c, 1728)]) for c in range(3)]
+    pairs = pairs[:1] + [(sel_hbm, sel), (pot_hbm, pot), (wh_hbm, wh), (wl_hbm, wl)] + pairs[1:]
+    loads = [pltpu.make_async_copy(a, b, in_sem.at[i]) for i, (a, b) in enumerate(pairs)]
     for load in loads:
         load.start()
 
@@ -133,17 +132,19 @@
             for i, (a, b, to) in enumerate(table)
         ]
 
-    def low_copy(slot):
-        return pltpu.make_async_remote_copy(
-            cen.at[slot, :, :, pl.ds(384, 384)], cen.at[slot, :, :, pl.ds(384 + CYZ, 384)],
-            send_sem.at[slot, 0, 4], recv_sem.at[slot, 0, 4], device_id=ends[1][0], device_id_type=MESH,
-        )
-
-    def high_copy(slot):
-        return pltpu.make_async_remote_copy(
-            cen.at[slot, :, :, pl.ds(CYZ, 384)], cen.at[slot, :, :, pl.ds(0, 384)],
-            send_sem.at[slot, 2, 4], recv_sem.at[slot, 2, 4], device_id=ends[1][1], device_id_type=MESH,
-        )
+    def y_copies(slot, m):
+        if m == 0:
+            table = ((cen.at[slot, :, :, pl.ds(384, 256)], cen.at[slot, :, :, pl.ds(384 + CYZ, 256)]), (ylo_out, yhi))
+        else:
+            table = ((cen.at[slot, :, :, pl.ds(128 + CYZ, 256)], cen.at[slot, :, :, pl.ds(128, 256)]), (yhi_out, ylo))
+        table = (table[0], (table[1][0].at[slot], table[1][1].at[slot]))
+        return [
+            pltpu.make_async_remote_copy(
+                a, b, send_sem.at[slot, m, 4 + i], recv_sem.at[slot, m, 4 + i],
+                device_id=ends[1][m // 2], device_id_type=MESH,
+            )
+            for i, (a, b) in enumerate(table)
+        ]
 
     def band_copy(chunk, m, half):
         part_of = (chunk, pl.ds(6 * half, 6), slice(None), pl.ds(768 * m, 768))
@@ -151,6 +152,8 @@
             fil.at[part_of], oth.at[part_of], band_send.at[chunk, m, half], band_recv.at[chunk, m, half],
             device_id=(1 - band, dom), device_id_type=MESH,
         )
+
+    lane = lax.broadcasted_iota(jnp.int32, (8, 128), 1)
 
     def group(i):
         return 2 * i % 3
@@ -162,20 +165,37 @@
         vh[slot, :, lanes] = high
         vl[slot, :, lanes] = low
         faces = dot(high, sel[...]) + dot(low, sel[...])
-        zlo_out[slot, :, :, face] = faces[:, :128].reshape(CX, 8, 128)
-        zhi_out[slot, :, :, face] = faces[:, 128:].reshape(CX, 8, 128)
+        for out, at in ((zlo_out, 0), (zhi_out, 128)):
+            f = faces[:, at : at + 128].reshape(CX, 8, 128)
+            for x in range(9):
+                last = pltpu.roll(f[x // 3 * 4 + 3], 96 - 32 * (x % 3), 1)
+                out[slot, x, :, face] = jnp.where(lane < 96, f[x // 3 * 4 + x % 3], last)
         for copy in copies(slot, m):
             copy.start()
 
+        def y_face(m, out, start, shift):
+            for g in range(3):
+                v = [cen[slot, 4 * g + q, :, pl.ds(start, 128)] for q in range(4)]
+                v = [pltpu.roll(v[q], (32 * q + shift) % 128, 1) for q in range(4)]
+                out[slot, g] = jnp.where(
+                    lane < 64, jnp.where(lane < 32, v[0], v[1]), jnp.where(lane < 96, v[2], v[3])
+                )
+            for copy in y_copies(slot, m):
+                copy.start()
+
         @pl.when(m == 0)
         def _():
-            low_copy(slot).start()
+            y_face(0, ylo_out, 640, 0)
 
         @pl.when(m == 2)
         def _():
-            high_copy(slot).start()
-
-    def split_rim(slot, start):
+            y_face(2, yhi_out, CYZ, 32)
+
+    def split_rim(slot, m, packed, start, at, shift):
+        for copy in y_copies(slot, m):
+            copy.wait_recv()
+        for x in range(CX):
+            cen[slot, x, :, pl.ds(at, 128)] = pltpu.roll(packed[slot, x // 4], (shift - 32 * (x % 4)) % 128, 1)
         high, low = split(cen[slot, :, :, pl.ds(start, 384)].reshape(96, 384))
         vh[slot, :, pl.ds(start, 384)] = high
         vl[slot, :, pl.ds(start, 384)] = low
@@ -186,17 +206,23 @@
 
         @pl.when(m == 0)
         def _():
-            high_copy(slot).wait_recv()
-            split_rim(slot, 0)
+            split_rim(slot, 2, ylo, 0, 0, 96)
 
         @pl.when(m == 2)
         def _():
-            low_copy(slot).wait_recv()
-            split_rim(slot, 384 + CYZ)
+            split_rim(slot, 0, yhi, 384 + CYZ, 640 + CYZ, 0)
+
+    def z_rim(rim, slot, face):
+        out = []
+        for g in range(3):
+            v = [rim[slot, 3 * g + q, :, face] for q in range(3)]
+            r = [pltpu.roll(v[q], 32 + 32 * q, 1) for q in range(3)]
+            out += v + [jnp.where(lane < 32, r[0], jnp.where(lane < 64, r[1], r[2]))]
+        return jnp.concatenate(out, 0)
 
     def yz_product(slot, m):
         face = pl.ds(pl.multiple_of(128 * m, 128), 128)
-        rims = jnp.concatenate([zlo[slot, :, :, face].reshape(96, 128), zhi[slot, :, :, face].reshape(96, 128)], 1)
+        rims = jnp.concatenate([z_rim(zlo, slot, face), z_rim(zhi, slot, face)], 1)
         zh, zl = split(rims)
         for j in range(3):
             window = pl.ds(pl.multiple_of(256 * j + 768 * m, 256), 1024)
@@ -226,19 +252,33 @@
                 lanes = pl.ds(pl.multiple_of(384 + 768 * m + 128 * t, 128), 128)
                 cen[chunk, x, :, lanes] = lin[pl.ds(row, 8, stride=216), :]
 
+    def rows(ref, m, first, layers):
+        lanes = pl.ds(pl.multiple_of(768 * m, 128), 768)
+        pieces = [split(ref[:, first + x, :, lanes].reshape(24, 768)) for x in range(layers)]
+        return jnp.concatenate([jnp.concatenate([p[i] for p in pieces], 1) for i in range(2)], 0)
+
+    def folded(a, b):
+        products = dot_t(a, b)
+        return products[:24, :24] + products[24:, :24] + products[:24, 24:]
+
+    def own_products(m):
+        a = rows(fil, m, 0, CX)
+        part[0, :, 0:24] += folded(a, a)
+
     def enter(chunk, m):
         relayout(chunk, m)
         prepare(chunk, m)
 
+    part[0] = jnp.zeros((24, 128), F32)
     loads[0].wait()
-    loads[4].wait()
+    loads[1].wait()
     pl.semaphore_wait(barrier, len(partners))
 
     @pl.loop(0, 3)
     def _(i):
         enter(0, group(i))
 
-    for load in loads[1:4]:
+    for load in loads[2:]:
         load.wait()
 
     @pl.loop(0, 3)
@@ -275,34 +315,21 @@
             def _():
                 band_copy(chunk, m, 0).start()
 
+            @pl.when(chunk == 2)
+            def _():
+                own_products(m)
+
         pltpu.make_async_copy(fil.at[chunk], f_hbm.at[chunk], out_sem.at[chunk]).start()
 
-    def rows(ref, x):
-        v = ref[:, x].reshape(24, CYZ)
-        high, low = split(v)
-        return jnp.concatenate([high, low], 0)
-
-    def folded(a, b):
-        products = dot_t(a, b)
-        return products[:24, :24] + products[24:, :24] + products[:24, 24:]
-
-    part[...] = jnp.zeros_like(part)
-
-    @pl.loop(0, CX)
-    def _(x):
-        a = rows(fil, x)
-        part[0, :, 0:24] += folded(a, a)
-
     part[0] = jnp.where(band == 0, part[0], pltpu.roll(part[0], 32, 1))
 
     @pl.loop(0, 3)
-    def _(chunk):
-        for m in range(3):
+    def _(i):
+        m = group(i)
+        for chunk in range(3):
             band_copy(chunk, m, band).wait_recv()
 
-    @pl.loop(0, 6)
-    def _(i):
-        mine, theirs = rows(fil, 6 * band + i), rows(oth, 6 * band + i)
+        mine, theirs = rows(fil, m, 6 * band, 6), rows(oth, m, 6 * band, 6)
         first, second = jnp.where(band == 0, mine, theirs), jnp.where(band == 0, theirs, mine)
         part[0, :, 64:88] += folded(second, first)
         part[0, :, 96:120] += folded(first, second)
@@ -353,8 +380,8 @@
         for m in range(3):
             for copy in copies(slot, m):
                 copy.wait_send()
-        low_copy(slot).wait_send()
-        high_copy(slot).wait_send()
+        for copy in y_copies(slot, 0) + y_copies(slot, 2):
+            copy.wait_send()
 
     @pl.loop(0, 3)
     def _(chunk):
@@ -392,10 +419,14 @@
             vm((6, CX, 8, LANES), F32),
             vm((6, 6, 8, CYZ), F32),
             vm((6, 6, 8, CYZ), F32),
-            vm((6, CX, 8, 384), F32),
-            vm((6, CX, 8, 384), F32),
-            vm((6, CX, 8, 384), F32),
-            vm((6, CX, 8, 384), F32),
+            vm((6, 9, 8, 384), F32),
+            vm((6, 9, 8, 384), F32),
+            vm((6, 9, 8, 384), F32),
+            vm((6, 9, 8, 384), F32),
+            vm((6, 3, 8, 128), F32),
+            vm((6, 3, 8, 128), F32),
+            vm((6, 3, 8, 128), F32),
+            vm((6, 3, 8, 128), F32),
             vm((6, 96, LANES), BF),
             vm((6, 96, LANES), BF),
             vm((96, 768), F32),
@@ -403,10 +434,10 @@
             vm(chunk, F32),
             vm((3, 24, 128), F32),
             vm((13, 24, 128), F32),
-            pltpu.SemaphoreType.DMA((5,)),
+            pltpu.SemaphoreType.DMA((7,)),
             pltpu.SemaphoreType.DMA((6,)),
-            pltpu.SemaphoreType.DMA((6, 3, 5)),
-            pltpu.SemaphoreType.DMA((6, 3, 5)),
+            pltpu.SemaphoreType.DMA((6, 3, 6)),
+            pltpu.SemaphoreType.DMA((6, 3, 6)),
             pltpu.SemaphoreType.DMA((3, 3, 2)),
             pltpu.SemaphoreType.DMA((3, 3, 2)),
             pltpu.SemaphoreType.DMA((13,)),

time: 121 us -> 116 us (0.959)
  Pallas kernels: 120 us -> 116 us
    pallas_call x1, Pallas kernels: 113 us -> 109 us  [filter_call(): pl.pallas_call(filter_kernel, out_shape=(jax.ShapeDtypeStruct(chunk, F32)...]
where the time goes in v3:
time: 116 us
  Pallas kernels  116 us (100%)
    pallas_call x1, Pallas kernels, filter_call(): pl.pallas_call(filter_kernel, out_shape=(jax.ShapeDtypeStruct(chunk, F32)...  109 us
    pallas_call x1, Pallas kernels, rotate_call(): pl.pallas_call(rotate_kernel, out_shape=jax.ShapeDtypeStruct((24, 216, 12...  7.15 us

profile of v3, /device:TPU:2, one launch (start us, length us, event | category | flops | bytes accessed | tf_op | source)
XLA Modules:
  0.0 116.0 jit_solution(11718540194462993075)
XLA Ops:
  0.0 108.8 %filter.1 = (f32[3,12,8,2304]{3,2,1,0:T(8,128)}, f32[3,12,8,2304]{3,2,1,0:T(8,128)}, f32[24,128]{1,0:T(8,128)}) custom-call(f32[5184,128]{1,0:T(8,128)} %bitcast.3, f32[216,128]{1,0:T(8,128)} %bitcast.4, bf16[3,1280,256]{2,1,0:T(8,128)(2,1)} %constant.6.clone.wh_hbm, bf16[3,1280,256]{2,1,0:T(8,128)(2,1)} %constant.7.clone.wl_hbm, ...), custom_call_target="tpu_custom_call" | custom-call | tf_op jit(solution)/shard_map/filter/pallas_call | solution.py:404
  108.8 7.1 %rotate.1 = f32[24,216,128]{2,1,0:T(8,128)} custom-call(f32[3,12,8,2304]{3,2,1,0:T(8,128)} %get-tuple-element.8.low, f32[3,12,8,2304]{3,2,1,0:T(8,128)} %get-tuple-element.9.high, f32[24,128]{1,0:T(8,128)} %get-tuple-element.10.gram), custom_call_target="tpu_custom_call" | custom-call | tf_op jit(solution)/shard_map/rotate/pallas_call | solution.py:523

commit v4 on v3

--- a/solution.py
+++ b/solution.py
@@ -83,8 +83,8 @@
 
 def filter_kernel(
     orb, pot_hbm, wh_hbm, wl_hbm, sel_hbm, f_hbm, fo_hbm, gram,
-    lin, pot, wh, wl, sel, cen, xlo, xhi, zlo, zhi, zlo_out, zhi_out, ylo, yhi, ylo_out, yhi_out, vh, vl, yz, fil, oth, part, got,
-    in_sem, out_sem, send_sem, recv_sem, band_send, band_recv, sum_send, sum_recv,
+    lin, pot, wh, wl, sel, cen, xrim, zlo, zhi, zlo_out, zhi_out, ylo, yhi, ylo_out, yhi_out, passed, vh, vl, yz, fil, oth, relay, part, got,
+    in_sem, out_sem, send_sem, recv_sem, y_send, y_recv, pass_send, hop_send, hop_recv, band_send, band_recv, sum_send, sum_recv,
 ):
     band, dom = lax.axis_index("band"), lax.axis_index("dom")
     pairs = [(orb.at[pl.ds(1728 * c, 1728)], lin.at[pl.ds(1728 * c, 1728)]) for c in range(3)]
@@ -101,30 +101,36 @@
         return (1 - band if other else band), to
 
     stages = [
-        [across(0, 0, 0, k % 2, k // 2) for k in range(1, 4)],
         [across(k // 2, k % 2, 0, 0, 0) for k in range(1, 8)],
-        [across(0, 0, k, 0, 0) for k in range(1, 4)],
+        [across(0, 0, k // 4, k // 2 % 2, k % 2) for k in range(1, 16)],
     ]
     partners = [partner for stage in stages for partner in stage]
     barrier = pltpu.get_barrier_semaphore()
     for partner in partners:
         pl.semaphore_signal(barrier, 1, device_id=partner, device_id_type=MESH)
 
-    ends = []
+    ends, odds = [], []
     for first in (1, 4, 16):
         odd = (dom // first % 4 + 1) // 2 % 2
         below = odd * flipped(dom, first) + (1 - odd) * flipped(dom, 2 * first)
         above = odd * flipped(dom, 2 * first) + (1 - odd) * flipped(dom, first)
         ends.append(((band, below), (band, above)))
+        odds.append(odd)
 
     def copies(slot, m):
-        lanes, centre, face = pl.ds(768 * m, 768), pl.ds(384 + 768 * m, 768), pl.ds(128 * m, 128)
-        table = (
-            (cen.at[slot, pl.ds(0, 6), :, centre], xhi.at[slot, :, :, lanes], ends[0][0]),
-            (cen.at[slot, pl.ds(6, 6), :, centre], xlo.at[slot, :, :, lanes], ends[0][1]),
+        face = pl.ds(128 * m, 128)
+        table = []
+        for part in range(2):
+            start = 768 * m + 384 * (part * odds[1] + (1 - part) * (1 - odds[1]))
+            lanes, centre = pl.ds(start, 384), pl.ds(384 + start, 384)
+            table += [
+                (cen.at[slot, pl.ds(0, 6), :, centre], xrim.at[slot, 1, :, :, lanes], ends[0][0]),
+                (cen.at[slot, pl.ds(6, 6), :, centre], xrim.at[slot, 0, :, :, lanes], ends[0][1]),
+            ]
+        table += [
             (zlo_out.at[slot, :, :, face], zhi.at[slot, :, :, face], ends[2][0]),
             (zhi_out.at[slot, :, :, face], zlo.at[slot, :, :, face], ends[2][1]),
-        )
+        ]
         return [
             pltpu.make_async_remote_copy(
                 a, b, send_sem.at[slot, m, i], recv_sem.at[slot, m, i], device_id=to, device_id_type=MESH
@@ -132,19 +138,27 @@
             for i, (a, b, to) in enumerate(table)
         ]
 
-    def y_copies(slot, m):
-        if m == 0:
-            table = ((cen.at[slot, :, :, pl.ds(384, 256)], cen.at[slot, :, :, pl.ds(384 + CYZ, 256)]), (ylo_out, yhi))
-        else:
-            table = ((cen.at[slot, :, :, pl.ds(128 + CYZ, 256)], cen.at[slot, :, :, pl.ds(128, 256)]), (yhi_out, ylo))
-        table = (table[0], (table[1][0].at[slot], table[1][1].at[slot]))
+    def y_moves(slot, face, half, sources, sems, to):
+        rim = cen.at[slot, pl.ds(6 * half, 6), :, pl.ds((384 + CYZ, 128)[face], 256)]
         return [
             pltpu.make_async_remote_copy(
-                a, b, send_sem.at[slot, m, 4 + i], recv_sem.at[slot, m, 4 + i],
-                device_id=ends[1][m // 2], device_id_type=MESH,
+                a, b, sems[i], y_recv.at[slot, face, half, i], device_id=to, device_id_type=MESH
             )
-            for i, (a, b) in enumerate(table)
+            for i, (a, b) in enumerate(zip(sources, (rim, (yhi, ylo)[face].at[slot, half])))
         ]
+
+    def y_copies(slot, face, half):
+        sources = (
+            cen.at[slot, pl.ds(6 * half, 6), :, pl.ds((384, 128 + CYZ)[face], 256)],
+            (ylo_out, yhi_out)[face].at[slot, half],
+        )
+        sems = [y_send.at[slot, face, half, i] for i in range(2)]
+        return y_moves(slot, face, half, sources, sems, ends[1][face])
+
+    def forward_copies(slot, face):
+        sources = (xrim.at[slot, odds[0], :, :, pl.ds((0, CYZ - 256)[face], 256)], passed.at[slot])
+        sems = [pass_send.at[slot, i] for i in range(2)]
+        return y_moves(slot, face, 1 - odds[0], sources, sems, (band, flipped(flipped(dom, 2), 4)))
 
     def band_copy(chunk, m, half):
         part_of = (chunk, pl.ds(6 * half, 6), slice(None), pl.ds(768 * m, 768))
@@ -153,10 +167,75 @@
             device_id=(1 - band, dom), device_id_type=MESH,
         )
 
+    far, near_by = (1 - band, flipped(dom, 32)), (1 - band, dom)
+
+    def hop(a, b, number, chunk, m, to):
+        return pltpu.make_async_remote_copy(
+            a, b, hop_send.at[number, chunk, m], hop_recv.at[number, chunk, m], device_id=to, device_id_type=MESH
+        )
+
+    def hops(number, chunk):
+        if number == 0:
+            return [
+                first_hop(chunk, m)
+                for m in range(3)
+            ]
+        if number == 1:
+            return [hop(relay.at[chunk], relay.at[chunk], 1, chunk, 0, near_by)]
+        return [hop(relay.at[chunk], oth.at[chunk, pl.ds(0, 6)], 2, chunk, 0, far)]
+
+    def first_hop(chunk, m):
+        at = pl.ds(pl.multiple_of(768 * m, 128), 768)
+        return hop(fil.at[chunk, pl.ds(0, 6), :, at], relay.at[chunk, :, :, at], 0, chunk, m, far)
+
+    def pass_on(number, chunk):
+        @pl.when(band == 2 - number)
+        def _():
+            for copy in hops(number - 1, chunk):
+                copy.wait_recv()
+            for copy in hops(number, chunk):
+                copy.start()
+
     lane = lax.broadcasted_iota(jnp.int32, (8, 128), 1)
 
     def group(i):
-        return 2 * i % 3
+        return 2 - i + odds[1] * (2 * i - 2)
+
+    def packed(tiles, shift):
+        v = [pltpu.roll(tile, (32 * (q % 4) + shift) % 128, 1) for q, tile in enumerate(tiles)]
+        first = jnp.where(lane < 64, jnp.where(lane < 32, v[0], v[1]), jnp.where(lane < 96, v[2], v[3]))
+        return first, jnp.where(lane < 32, v[4], v[5])
+
+    def for_outer(face, act):
+        @pl.when(odds[1] == face)
+        def _():
+            act()
+
+    def send_y(slot, face):
+        start, shift = ((640, 0), (CYZ, 32))[face]
+        for half in range(2):
+            tiles = [cen[slot, 6 * half + q, :, pl.ds(start, 128)] for q in range(6)]
+            out = (ylo_out, yhi_out)[face]
+            out[slot, half, 0], out[slot, half, 1] = packed(tiles, shift)
+
+        def start_outer():
+            for copy in y_copies(slot, face, odds[0]):
+                copy.start()
+
+        for copy in y_copies(slot, face, 1 - odds[0]):
+            copy.start()
+        for_outer(face, start_outer)
+
+    def forward(slot):
+        for face in range(2):
+
+            @pl.when(odds[1] == 1 - face)
+            def _():
+                start, shift = ((256, 0), (CYZ - 384, 32))[face]
+                tiles = [xrim[slot, odds[0], q, :, pl.ds(start, 128)] for q in range(6)]
+                passed[slot, 0], passed[slot, 1] = packed(tiles, shift)
+                for copy in forward_copies(slot, face):
+                    copy.start()
 
     def prepare(slot, m):
         lanes = pl.ds(pl.multiple_of(384 + 768 * m, 128), 768)
@@ -170,47 +249,49 @@
             for x in range(9):
                 last = pltpu.roll(f[x // 3 * 4 + 3], 96 - 32 * (x % 3), 1)
                 out[slot, x, :, face] = jnp.where(lane < 96, f[x // 3 * 4 + x % 3], last)
-        for copy in copies(slot, m):
+
+    def send(slot, m, first, count):
+        for copy in copies(slot, m)[first : first + count]:
             copy.start()
 
-        def y_face(m, out, start, shift):
-            for g in range(3):
-                v = [cen[slot, 4 * g + q, :, pl.ds(start, 128)] for q in range(4)]
-                v = [pltpu.roll(v[q], (32 * q + shift) % 128, 1) for q in range(4)]
-                out[slot, g] = jnp.where(
-                    lane < 64, jnp.where(lane < 32, v[0], v[1]), jnp.where(lane < 96, v[2], v[3])
-                )
-            for copy in y_copies(slot, m):
-                copy.start()
-
-        @pl.when(m == 0)
-        def _():
-            y_face(0, ylo_out, 640, 0)
-
-        @pl.when(m == 2)
-        def _():
-            y_face(2, yhi_out, CYZ, 32)
-
-    def split_rim(slot, m, packed, start, at, shift):
-        for copy in y_copies(slot, m):
-            copy.wait_recv()
+    def split_rim(slot, face, rim, start, at, shift):
+        for half in range(2):
+            for copy in y_copies(slot, face, half):
+                copy.wait_recv()
         for x in range(CX):
-            cen[slot, x, :, pl.ds(at, 128)] = pltpu.roll(packed[slot, x // 4], (shift - 32 * (x % 4)) % 128, 1)
+            tile = rim[slot, x // 6, x % 6 // 4]
+            cen[slot, x, :, pl.ds(at, 128)] = pltpu.roll(tile, (shift - 32 * (x % 6 % 4)) % 128, 1)
         high, low = split(cen[slot, :, :, pl.ds(start, 384)].reshape(96, 384))
         vh[slot, :, pl.ds(start, 384)] = high
         vl[slot, :, pl.ds(start, 384)] = low
 
-    def receive(slot, m):
-        for copy in copies(slot, m):
+    def receive_y(slot, m):
+        @pl.when(m == 0)
+        def _():
+            split_rim(slot, 1, ylo, 0, 0, 96)
+
+        @pl.when(m == 2)
+        def _():
+            split_rim(slot, 0, yhi, 384 + CYZ, 640 + CYZ, 0)
+
+    def receive(slot, m, first, count):
+        for copy in copies(slot, m)[first : first + count]:
             copy.wait_recv()
 
-        @pl.when(m == 0)
-        def _():
-            split_rim(slot, 2, ylo, 0, 0, 96)
-
-        @pl.when(m == 2)
-        def _():
-            split_rim(slot, 0, yhi, 384 + CYZ, 640 + CYZ, 0)
+    def arrive(slot, m, i):
+        @pl.when(i == 0)
+        def _():
+            receive(slot, m, 0, 2)
+            forward(slot)
+
+        receive_y(slot, m)
+        yz_product(slot, m)
+
+        @pl.when(i > 0)
+        def _():
+            receive(slot, m, 0, 2)
+
+        receive(slot, m, 2, 4)
 
     def z_rim(rim, slot, face):
         out = []
@@ -221,23 +302,27 @@
         return jnp.concatenate(out, 0)
 
     def yz_product(slot, m):
-        face = pl.ds(pl.multiple_of(128 * m, 128), 128)
-        rims = jnp.concatenate([z_rim(zlo, slot, face), z_rim(zhi, slot, face)], 1)
-        zh, zl = split(rims)
         for j in range(3):
             window = pl.ds(pl.multiple_of(256 * j + 768 * m, 256), 1024)
-            high = jnp.concatenate([vh[slot, :, window], zh], 1)
-            low = jnp.concatenate([vl[slot, :, window], zl], 1)
-            yz[:, pl.ds(256 * j, 256)] = dot(high, wh[j]) + dot(low, wh[j]) + dot(high, wl[j])
+            high, low = vh[slot, :, window], vl[slot, :, window]
+            wide = dot(high, wh[j, 0:1024]) + dot(low, wh[j, 0:1024]) + dot(high, wl[j, 0:1024])
+            yz[:, pl.ds(256 * j, 256)] = wide
+
+    def rim_product(slot, m):
+        face = pl.ds(pl.multiple_of(128 * m, 128), 128)
+        high, low = split(jnp.concatenate([z_rim(zlo, slot, face), z_rim(zhi, slot, face)], 1))
+        for j in range(3):
+            rims = slice(1024, 1280)
+            yz[:, pl.ds(256 * j, 256)] += dot(high, wh[j, rims]) + dot(low, wh[j, rims]) + dot(high, wl[j, rims])
 
     def stencil(slot, m, write):
         @pl.loop(0, 6)
         def _(t):
             at = pl.multiple_of(768 * m + 128 * t, 128)
             here, mid = pl.ds(at, 128), pl.ds(pl.multiple_of(at + 384, 128), 128)
-            v = [xlo[slot, i, :, here] for i in range(6)]
+            v = [xrim[slot, 0, i, :, here] for i in range(6)]
             v += [cen[slot, i, :, mid] for i in range(CX)]
-            v += [xhi[slot, i, :, here] for i in range(6)]
+            v += [xrim[slot, 1, i, :, here] for i in range(6)]
             for x in range(CX):
                 diagonal = pot[pl.ds(18 * x + 6 * m + t, 1), :] * (1.0 / half_width) + own
                 total = diagonal * v[x + 6] + yz[pl.ds(8 * x, 8), pl.ds(pl.multiple_of(128 * t, 128), 128)]
@@ -265,18 +350,28 @@
         a = rows(fil, m, 0, CX)
         part[0, :, 0:24] += folded(a, a)
 
-    def enter(chunk, m):
-        relayout(chunk, m)
-        prepare(chunk, m)
+    def enter(chunk):
+        @pl.loop(0, 3)
+        def _(i):
+            relayout(chunk, group(i))
 
     part[0] = jnp.zeros((24, 128), F32)
     loads[0].wait()
     loads[1].wait()
     pl.semaphore_wait(barrier, len(partners))
+    enter(0)
+    send(0, group(0), 0, 4)
+    send_y(0, 0)
+    send_y(0, 1)
 
     @pl.loop(0, 3)
     def _(i):
-        enter(0, group(i))
+        @pl.when(i > 0)
+        def _():
+            send(0, group(i), 0, 4)
+
+        prepare(0, group(i))
+        send(0, group(i), 4, 2)
 
     for load in loads[2:]:
         load.wait()
@@ -285,35 +380,62 @@
     def _(chunk):
         @pl.loop(0, 3)
         def _(i):
-            m = group(i)
-            receive(chunk, m)
+            m, slot = group(i), chunk
+            arrive(slot, m, i)
+            rim_product(slot, m)
 
             def write(x, here, mid, total):
                 cen[chunk + 3, x, :, mid] = total
 
-            yz_product(chunk, m)
-            stencil(chunk, m, write)
-            prepare(chunk + 3, m)
+            stencil(slot, m, write)
+
+            send(slot + 3, m, 0, 4)
+
+            @pl.when(m == 0)
+            def _():
+                send_y(slot + 3, 0)
+
+            @pl.when(m == 2)
+            def _():
+                send_y(slot + 3, 1)
+
+            prepare(slot + 3, m)
+            send(slot + 3, m, 4, 2)
+
+        @pl.when(chunk > 0)
+        def _():
+            pass_on(1, chunk - 1)
+
+        @pl.when(chunk < 2)
+        def _():
+            enter(chunk + 1)
+            send_y(chunk + 1, 0)
+            send_y(chunk + 1, 1)
+
+            @pl.loop(0, 3)
+            def _(i):
+                prepare(chunk + 1, group(i))
 
         @pl.loop(0, 3)
         def _(i):
-            m = group(i)
-            receive(chunk + 3, m)
+            m, slot = group(i), chunk + 3
+            arrive(slot, m, i)
 
             @pl.when(chunk < 2)
             def _():
-                enter(chunk + 1, m)
+                send(chunk + 1, m, 0, 6)
+
+            rim_product(slot, m)
 
             def write(x, here, mid, total):
                 fil[chunk, x, :, here] = 2.0 * total - cen[chunk, x, :, mid]
 
-            yz_product(chunk + 3, m)
-            stencil(chunk + 3, m, write)
+            stencil(slot, m, write)
             band_copy(chunk, m, 1 - band).start()
 
             @pl.when((band == 0) & (chunk < 2))
             def _():
-                band_copy(chunk, m, 0).start()
+                first_hop(chunk, m).start()
 
             @pl.when(chunk == 2)
             def _():
@@ -321,18 +443,33 @@
 
         pltpu.make_async_copy(fil.at[chunk], f_hbm.at[chunk], out_sem.at[chunk]).start()
 
+        @pl.when(chunk > 0)
+        def _():
+            pass_on(2, chunk - 1)
+
     part[0] = jnp.where(band == 0, part[0], pltpu.roll(part[0], 32, 1))
 
-    @pl.loop(0, 3)
-    def _(i):
-        m = group(i)
+    def cross_products(m):
         for chunk in range(3):
             band_copy(chunk, m, band).wait_recv()
-
         mine, theirs = rows(fil, m, 6 * band, 6), rows(oth, m, 6 * band, 6)
         first, second = jnp.where(band == 0, mine, theirs), jnp.where(band == 0, theirs, mine)
         part[0, :, 64:88] += folded(second, first)
         part[0, :, 96:120] += folded(first, second)
+
+    @pl.loop(0, 3)
+    def _(i):
+        @pl.when(i == 2)
+        def _():
+            for m in range(3):
+                band_copy(2, m, 1 - band).wait_send()
+
+            @pl.when(band == 0)
+            def _():
+                for m in range(3):
+                    band_copy(2, m, 0).start()
+
+        cross_products(group(i))
 
     index = 0
     for number, stage in enumerate(stages):
@@ -348,17 +485,10 @@
             index += 1
         for move in moves:
             move.wait_recv()
-        if number == 0:
-
-            @pl.when(band == 0)
-            def _():
-                for m in range(3):
-                    band_copy(2, m, 0).start()
-
         terms = [part[number]] + [got[index - len(stage) + k] for k in range(len(stage))]
         while len(terms) > 1:
             terms = [a + b for a, b in zip(terms[::2], terms[1::2])]
-        if number < 2:
+        if number < 1:
             part[number + 1] = terms[0]
         else:
             gram[...] = terms[0]
@@ -369,8 +499,18 @@
     def _():
         @pl.loop(0, 3)
         def _(chunk):
-            for m in range(3):
-                band_copy(chunk, m, 0).wait_recv()
+            @pl.when(chunk < 2)
+            def _():
+                for copy in hops(2, chunk):
+                    copy.wait_recv()
+                for copy in hops(1, chunk):
+                    copy.wait_send()
+
+            @pl.when(chunk == 2)
+            def _():
+                for m in range(3):
+                    band_copy(2, m, 0).wait_recv()
+
             copy = pltpu.make_async_copy(oth.at[chunk], fo_hbm.at[chunk], out_sem.at[3 + chunk])
             copy.start()
             copy.wait()
@@ -380,17 +520,34 @@
         for m in range(3):
             for copy in copies(slot, m):
                 copy.wait_send()
-        for copy in y_copies(slot, 0) + y_copies(slot, 2):
+        for face in range(2):
+
+            def wait_outer():
+                for copy in y_copies(slot, face, odds[0]):
+                    copy.wait_send()
+
+            for copy in y_copies(slot, face, 1 - odds[0]):
+                copy.wait_send()
+            for_outer(face, wait_outer)
+        for copy in forward_copies(slot, 0):
             copy.wait_send()
 
     @pl.loop(0, 3)
     def _(chunk):
-        for m in range(3):
-            band_copy(chunk, m, 1 - band).wait_send()
+        @pl.when(chunk < 2)
+        def _():
+            for m in range(3):
+                band_copy(chunk, m, 1 - band).wait_send()
 
             @pl.when(band == 0)
             def _():
-                band_copy(chunk, m, 0).wait_send()
+                for copy in hops(0, chunk) + hops(2, chunk):
+                    copy.wait_send()
+
+        @pl.when((band == 0) & (chunk == 2))
+        def _():
+            for m in range(3):
+                band_copy(2, m, 0).wait_send()
 
         pltpu.make_async_copy(fil.at[chunk], f_hbm.at[chunk], out_sem.at[chunk]).wait()
 
@@ -417,31 +574,37 @@
             vm(wl.shape, BF),
             vm(sel.shape, BF),
             vm((6, CX, 8, LANES), F32),
-            vm((6, 6, 8, CYZ), F32),
-            vm((6, 6, 8, CYZ), F32),
+            vm((6, 2, 6, 8, CYZ), F32),
             vm((6, 9, 8, 384), F32),
             vm((6, 9, 8, 384), F32),
             vm((6, 9, 8, 384), F32),
             vm((6, 9, 8, 384), F32),
-            vm((6, 3, 8, 128), F32),
-            vm((6, 3, 8, 128), F32),
-            vm((6, 3, 8, 128), F32),
-            vm((6, 3, 8, 128), F32),
+            vm((6, 2, 2, 8, 128), F32),
+            vm((6, 2, 2, 8, 128), F32),
+            vm((6, 2, 2, 8, 128), F32),
+            vm((6, 2, 2, 8, 128), F32),
+            vm((6, 2, 8, 128), F32),
             vm((6, 96, LANES), BF),
             vm((6, 96, LANES), BF),
             vm((96, 768), F32),
             vm(chunk, F32),
             vm(chunk, F32),
-            vm((3, 24, 128), F32),
-            vm((13, 24, 128), F32),
+            vm((2, 6, 8, CYZ), F32),
+            vm((2, 24, 128), F32),
+            vm((22, 24, 128), F32),
             pltpu.SemaphoreType.DMA((7,)),
             pltpu.SemaphoreType.DMA((6,)),
             pltpu.SemaphoreType.DMA((6, 3, 6)),
             pltpu.SemaphoreType.DMA((6, 3, 6)),
+            pltpu.SemaphoreType.DMA((6, 2, 2, 2)),
+            pltpu.SemaphoreType.DMA((6, 2, 2, 2)),
+            pltpu.SemaphoreType.DMA((6, 2)),
+            pltpu.SemaphoreType.DMA((3, 2, 3)),
+            pltpu.SemaphoreType.DMA((3, 2, 3)),
             pltpu.SemaphoreType.DMA((3, 3, 2)),
             pltpu.SemaphoreType.DMA((3, 3, 2)),
-            pltpu.SemaphoreType.DMA((13,)),
-            pltpu.SemaphoreType.DMA((13,)),
+            pltpu.SemaphoreType.DMA((22,)),
+            pltpu.SemaphoreType.DMA((22,)),
         ],
         compiler_params=pltpu.CompilerParams(collective_id=0, has_side_effects=True, vmem_limit_bytes=56 << 20),
         name="filter",

time: 116 us -> 111 us (0.957)
  Pallas kernels: 116 us -> 111 us
    pallas_call x1, Pallas kernels: 109 us -> 104 us  [filter_call(): pl.pallas_call(filter_kernel, out_shape=(jax.ShapeDtypeStruct(chunk, F32)...]
where the time goes in v4:
time: 111 us
  Pallas kernels  111 us (100%)
    pallas_call x1, Pallas kernels, filter_call(): pl.pallas_call(filter_kernel, out_shape=(jax.ShapeDtypeStruct(chunk, F32)...  104 us
    pallas_call x1, Pallas kernels, rotate_call(): pl.pallas_call(rotate_kernel, out_shape=jax.ShapeDtypeStruct((24, 216, 12...  7.15 us

profile of v4, /device:TPU:2, one launch (start us, length us, event | category | flops | bytes accessed | tf_op | source)
XLA Modules:
  0.0 111.2 jit_solution(5926540492912624203)
XLA Ops:
  0.0 104.0 %filter.1 = (f32[3,12,8,2304]{3,2,1,0:T(8,128)}, f32[3,12,8,2304]{3,2,1,0:T(8,128)}, f32[24,128]{1,0:T(8,128)}) custom-call(f32[5184,128]{1,0:T(8,128)} %bitcast.3, f32[216,128]{1,0:T(8,128)} %bitcast.4, bf16[3,1280,256]{2,1,0:T(8,128)(2,1)} %constant.6.clone.wh_hbm, bf16[3,1280,256]{2,1,0:T(8,128)(2,1)} %constant.7.clone.wl_hbm, ...), custom_call_target="tpu_custom_call" | custom-call | tf_op jit(solution)/shard_map/filter/pallas_call | solution.py:561
  104.0 7.1 %rotate.1 = f32[24,216,128]{2,1,0:T(8,128)} custom-call(f32[3,12,8,2304]{3,2,1,0:T(8,128)} %get-tuple-element.8.low, f32[3,12,8,2304]{3,2,1,0:T(8,128)} %get-tuple-element.9.high, f32[24,128]{1,0:T(8,128)} %get-tuple-element.10.gram), custom_call_target="tpu_custom_call" | custom-call | tf_op jit(solution)/shard_map/rotate/pallas_call | solution.py:686

commit v5 on v4

--- a/solution.py
+++ b/solution.py
@@ -83,8 +83,8 @@
 
 def filter_kernel(
     orb, pot_hbm, wh_hbm, wl_hbm, sel_hbm, f_hbm, fo_hbm, gram,
-    lin, pot, wh, wl, sel, cen, xrim, zlo, zhi, zlo_out, zhi_out, ylo, yhi, ylo_out, yhi_out, passed, vh, vl, yz, fil, oth, relay, part, got,
-    in_sem, out_sem, send_sem, recv_sem, y_send, y_recv, pass_send, hop_send, hop_recv, band_send, band_recv, sum_send, sum_recv,
+    lin, pot, wh, wl, sel, cen, xrim, zlo, zhi, zlo_out, zhi_out, ylo, yhi, ylo_out, yhi_out, passed, vh, vl, yz, fil, oth, part, got,
+    in_sem, out_sem, send_sem, recv_sem, y_send, y_recv, pass_send, band_send, band_recv, sum_send, sum_recv,
 ):
     band, dom = lax.axis_index("band"), lax.axis_index("dom")
     pairs = [(orb.at[pl.ds(1728 * c, 1728)], lin.at[pl.ds(1728 * c, 1728)]) for c in range(3)]
@@ -167,35 +167,6 @@
             device_id=(1 - band, dom), device_id_type=MESH,
         )
 
-    far, near_by = (1 - band, flipped(dom, 32)), (1 - band, dom)
-
-    def hop(a, b, number, chunk, m, to):
-        return pltpu.make_async_remote_copy(
-            a, b, hop_send.at[number, chunk, m], hop_recv.at[number, chunk, m], device_id=to, device_id_type=MESH
-        )
-
-    def hops(number, chunk):
-        if number == 0:
-            return [
-                first_hop(chunk, m)
-                for m in range(3)
-            ]
-        if number == 1:
-            return [hop(relay.at[chunk], relay.at[chunk], 1, chunk, 0, near_by)]
-        return [hop(relay.at[chunk], oth.at[chunk, pl.ds(0, 6)], 2, chunk, 0, far)]
-
-    def first_hop(chunk, m):
-        at = pl.ds(pl.multiple_of(768 * m, 128), 768)
-        return hop(fil.at[chunk, pl.ds(0, 6), :, at], relay.at[chunk, :, :, at], 0, chunk, m, far)
-
-    def pass_on(number, chunk):
-        @pl.when(band == 2 - number)
-        def _():
-            for copy in hops(number - 1, chunk):
-                copy.wait_recv()
-            for copy in hops(number, chunk):
-                copy.start()
-
     lane = lax.broadcasted_iota(jnp.int32, (8, 128), 1)
 
     def group(i):
@@ -278,7 +249,7 @@
         for copy in copies(slot, m)[first : first + count]:
             copy.wait_recv()
 
-    def arrive(slot, m, i):
+    def arrive(slot, m, i, meanwhile):
         @pl.when(i == 0)
         def _():
             receive(slot, m, 0, 2)
@@ -286,6 +257,7 @@
 
         receive_y(slot, m)
         yz_product(slot, m)
+        meanwhile()
 
         @pl.when(i > 0)
         def _():
@@ -355,11 +327,18 @@
         def _(i):
             relayout(chunk, group(i))
 
+        if chunk > 0:
+
+            @pl.loop(0, 3)
+            def _(i):
+                prepare(chunk, group(i))
+                send(chunk, group(i), 4, 2)
+
     part[0] = jnp.zeros((24, 128), F32)
     loads[0].wait()
     loads[1].wait()
+    enter(0)
     pl.semaphore_wait(barrier, len(partners))
-    enter(0)
     send(0, group(0), 0, 4)
     send_y(0, 0)
     send_y(0, 1)
@@ -375,13 +354,20 @@
 
     for load in loads[2:]:
         load.wait()
+    enter(1)
 
     @pl.loop(0, 3)
     def _(chunk):
         @pl.loop(0, 3)
         def _(i):
             m, slot = group(i), chunk
-            arrive(slot, m, i)
+
+            def meanwhile():
+                @pl.when((band == 0) & (chunk > 0))
+                def _():
+                    band_copy(chunk - 1, m, 0).start()
+
+            arrive(slot, m, i, meanwhile)
             rim_product(slot, m)
 
             def write(x, here, mid, total):
@@ -402,28 +388,23 @@
             prepare(slot + 3, m)
             send(slot + 3, m, 4, 2)
 
-        @pl.when(chunk > 0)
-        def _():
-            pass_on(1, chunk - 1)
+        @pl.when(chunk == 0)
+        def _():
+            enter(2)
 
         @pl.when(chunk < 2)
         def _():
-            enter(chunk + 1)
             send_y(chunk + 1, 0)
             send_y(chunk + 1, 1)
-
-            @pl.loop(0, 3)
-            def _(i):
-                prepare(chunk + 1, group(i))
 
         @pl.loop(0, 3)
         def _(i):
             m, slot = group(i), chunk + 3
-            arrive(slot, m, i)
+            arrive(slot, m, i, lambda: None)
 
             @pl.when(chunk < 2)
             def _():
-                send(chunk + 1, m, 0, 6)
+                send(chunk + 1, m, 0, 4)
 
             rim_product(slot, m)
 
@@ -432,20 +413,12 @@
 
             stencil(slot, m, write)
             band_copy(chunk, m, 1 - band).start()
-
-            @pl.when((band == 0) & (chunk < 2))
-            def _():
-                first_hop(chunk, m).start()
 
             @pl.when(chunk == 2)
             def _():
                 own_products(m)
 
         pltpu.make_async_copy(fil.at[chunk], f_hbm.at[chunk], out_sem.at[chunk]).start()
-
-        @pl.when(chunk > 0)
-        def _():
-            pass_on(2, chunk - 1)
 
     part[0] = jnp.where(band == 0, part[0], pltpu.roll(part[0], 32, 1))
 
@@ -499,18 +472,8 @@
     def _():
         @pl.loop(0, 3)
         def _(chunk):
-            @pl.when(chunk < 2)
-            def _():
-                for copy in hops(2, chunk):
-                    copy.wait_recv()
-                for copy in hops(1, chunk):
-                    copy.wait_send()
-
-            @pl.when(chunk == 2)
-            def _():
-                for m in range(3):
-                    band_copy(2, m, 0).wait_recv()
-
+            for m in range(3):
+                band_copy(chunk, m, 0).wait_recv()
             copy = pltpu.make_async_copy(oth.at[chunk], fo_hbm.at[chunk], out_sem.at[3 + chunk])
             copy.start()
             copy.wait()
@@ -539,15 +502,10 @@
             for m in range(3):
                 band_copy(chunk, m, 1 - band).wait_send()
 
-            @pl.when(band == 0)
-            def _():
-                for copy in hops(0, chunk) + hops(2, chunk):
-                    copy.wait_send()
-
-        @pl.when((band == 0) & (chunk == 2))
+        @pl.when(band == 0)
         def _():
             for m in range(3):
-                band_copy(2, m, 0).wait_send()
+                band_copy(chunk, m, 0).wait_send()
 
         pltpu.make_async_copy(fil.at[chunk], f_hbm.at[chunk], out_sem.at[chunk]).wait()
 
@@ -589,7 +547,6 @@
             vm((96, 768), F32),
             vm(chunk, F32),
             vm(chunk, F32),
-            vm((2, 6, 8, CYZ), F32),
             vm((2, 24, 128), F32),
             vm((22, 24, 128), F32),
             pltpu.SemaphoreType.DMA((7,)),
@@ -599,8 +556,6 @@
             pltpu.SemaphoreType.DMA((6, 2, 2, 2)),
             pltpu.SemaphoreType.DMA((6, 2, 2, 2)),
             pltpu.SemaphoreType.DMA((6, 2)),
-            pltpu.SemaphoreType.DMA((3, 2, 3)),
-            pltpu.SemaphoreType.DMA((3, 2, 3)),
             pltpu.SemaphoreType.DMA((3, 3, 2)),
             pltpu.SemaphoreType.DMA((3, 3, 2)),
             pltpu.SemaphoreType.DMA((22,)),
@@ -656,13 +611,14 @@
 
     def rotate(matrix, sources):
         mh, ml = split(matrix)
-        left = jnp.concatenate([mh, ml, mh], 1)
+        left = jnp.concatenate([jnp.concatenate([mh, mh], 1), jnp.concatenate([ml, jnp.zeros_like(ml)], 1)], 0)
         for x in range(CX):
             for load in loads(x)[: len(sources)]:
                 load.wait()
             v = [source[:, x].reshape(24, CYZ) for source in sources]
             vh, vl = split(jnp.concatenate(v, 0) if len(v) > 1 else v[0])
-            made = dot(left, jnp.concatenate([vh, vh, vl], 0))
+            made = dot(left, jnp.concatenate([vh, vl], 0))
+            made = made[:24] + made[24:]
             for t in range(18):
                 lines[pl.ds(18 * x + t, 24, stride=216), :] = made[:, 128 * t : 128 * t + 128]
             if x % 4 == 3:

time: 111 us -> 107 us (0.964)
  Pallas kernels: 111 us -> 107 us
    pallas_call x1, Pallas kernels: 104 us -> 99.8 us  [filter_call(): pl.pallas_call(filter_kernel, out_shape=(jax.ShapeDtypeStruct(chunk, F32)...]
where the time goes in v5:
time: 107 us
  Pallas kernels  107 us (100%)
    pallas_call x1, Pallas kernels, filter_call(): pl.pallas_call(filter_kernel, out_shape=(jax.ShapeDtypeStruct(chunk, F32)...  99.8 us
    pallas_call x1, Pallas kernels, rotate_call(): pl.pallas_call(rotate_kernel, out_shape=jax.ShapeDtypeStruct((24, 216, 12...  6.84 us

profile of v5, /device:TPU:2, one launch (start us, length us, event | category | flops | bytes accessed | tf_op | source)
XLA Modules:
  0.0 106.7 jit_solution(14237123868724221911)
XLA Ops:
  0.0 99.8 %filter.1 = (f32[3,12,8,2304]{3,2,1,0:T(8,128)}, f32[3,12,8,2304]{3,2,1,0:T(8,128)}, f32[24,128]{1,0:T(8,128)}) custom-call(f32[5184,128]{1,0:T(8,128)} %bitcast.3, f32[216,128]{1,0:T(8,128)} %bitcast.4, bf16[3,1280,256]{2,1,0:T(8,128)(2,1)} %constant.6.clone.wh_hbm, bf16[3,1280,256]{2,1,0:T(8,128)(2,1)} %constant.7.clone.wl_hbm, ...), custom_call_target="tpu_custom_call" | custom-call | tf_op jit(solution)/shard_map/filter/pallas_call | solution.py:519
  99.8 6.8 %rotate.1 = f32[24,216,128]{2,1,0:T(8,128)} custom-call(f32[3,12,8,2304]{3,2,1,0:T(8,128)} %get-tuple-element.8.low, f32[3,12,8,2304]{3,2,1,0:T(8,128)} %get-tuple-element.9.high, f32[24,128]{1,0:T(8,128)} %get-tuple-element.10.gram), custom_call_target="tpu_custom_call" | custom-call | tf_op jit(solution)/shard_map/rotate/pallas_call | solution.py:642

commit v6 on v5

--- a/solution.py
+++ b/solution.py
@@ -83,7 +83,7 @@
 
 def filter_kernel(
     orb, pot_hbm, wh_hbm, wl_hbm, sel_hbm, f_hbm, fo_hbm, gram,
-    lin, pot, wh, wl, sel, cen, xrim, zlo, zhi, zlo_out, zhi_out, ylo, yhi, ylo_out, yhi_out, passed, vh, vl, yz, fil, oth, part, got,
+    lin, pot, wh, wl, sel, cen, xrim, zlo, zhi, zlo_out, zhi_out, ylo, yhi, ylo_out, yhi_out, passed, vh, vl, yz, fil, oth, acc, part, got,
     in_sem, out_sem, send_sem, recv_sem, y_send, y_recv, pass_send, band_send, band_recv, sum_send, sum_recv,
 ):
     band, dom = lax.axis_index("band"), lax.axis_index("dom")
@@ -320,7 +320,7 @@
 
     def own_products(m):
         a = rows(fil, m, 0, CX)
-        part[0, :, 0:24] += folded(a, a)
+        acc[:, 0:24] += folded(a, a)
 
     def enter(chunk):
         @pl.loop(0, 3)
@@ -334,7 +334,7 @@
                 prepare(chunk, group(i))
                 send(chunk, group(i), 4, 2)
 
-    part[0] = jnp.zeros((24, 128), F32)
+    acc[...] = jnp.zeros_like(acc)
     loads[0].wait()
     loads[1].wait()
     enter(0)
@@ -420,15 +420,12 @@
 
         pltpu.make_async_copy(fil.at[chunk], f_hbm.at[chunk], out_sem.at[chunk]).start()
 
-    part[0] = jnp.where(band == 0, part[0], pltpu.roll(part[0], 32, 1))
-
     def cross_products(m):
         for chunk in range(3):
             band_copy(chunk, m, band).wait_recv()
         mine, theirs = rows(fil, m, 6 * band, 6), rows(oth, m, 6 * band, 6)
         first, second = jnp.where(band == 0, mine, theirs), jnp.where(band == 0, theirs, mine)
-        part[0, :, 64:88] += folded(second, first)
-        part[0, :, 96:120] += folded(first, second)
+        acc[:, 64:88] += folded(second, first)
 
     @pl.loop(0, 3)
     def _(i):
@@ -443,6 +440,16 @@
                     band_copy(2, m, 0).start()
 
         cross_products(group(i))
+
+    v = acc[...]
+    alone = jnp.where(lax.broadcasted_iota(jnp.int32, (24, 128), 1) < 24, v, 0.0)
+    cross = v - alone
+    tail = pltpu.roll(alone[16:], 72, 1)
+    part[0] = (
+        jnp.where(band == 0, alone[:16], pltpu.roll(alone[:16], 24, 1))
+        + pltpu.roll(cross[:16], 112, 1)
+        + jnp.concatenate([jnp.where(band == 0, tail, 0.0) + pltpu.roll(cross[16:], 32, 1), jnp.where(band == 0, 0.0, tail)], 0)
+    )
 
     index = 0
     for number, stage in enumerate(stages):
@@ -454,8 +461,9 @@
                     device_id=partner, device_id_type=MESH,
                 )
             )
-            moves[-1].start()
             index += 1
+        for move in moves:
+            move.start()
         for move in moves:
             move.wait_recv()
         terms = [part[number]] + [got[index - len(stage) + k] for k in range(len(stage))]
@@ -521,7 +529,7 @@
         out_shape=(
             jax.ShapeDtypeStruct(chunk, F32),
             jax.ShapeDtypeStruct(chunk, F32),
-            jax.ShapeDtypeStruct((24, 128), F32),
+            jax.ShapeDtypeStruct((16, 128), F32),
         ),
         in_specs=[any_space] * 5,
         out_specs=(any_space, any_space, pl.BlockSpec(memory_space=pltpu.VMEM)),
@@ -547,8 +555,9 @@
             vm((96, 768), F32),
             vm(chunk, F32),
             vm(chunk, F32),
-            vm((2, 24, 128), F32),
-            vm((22, 24, 128), F32),
+            vm((24, 128), F32),
+            vm((2, 16, 128), F32),
+            vm((22, 16, 128), F32),
             pltpu.SemaphoreType.DMA((7,)),
             pltpu.SemaphoreType.DMA((6,)),
             pltpu.SemaphoreType.DMA((6, 3, 6)),
@@ -583,10 +592,15 @@
     g = gram[...] * (1.0 / (64 * CX * CYZ))
     blank = jnp.zeros((24, 16), F32)
     row, col = (lax.broadcasted_iota(jnp.int32, (48, 64), d) for d in range(2))
+    unit = (row == col).astype(F32)
+    first = jnp.concatenate([g[:, 0:24], g[0:8, 72:96]], 0)
+    second = jnp.concatenate([g[:, 24:48], g[8:16, 72:96]], 0)
+    cross = jnp.concatenate([g[:, 48:72], g[0:8, 96:120]], 0)
+    turned = lax.dot_general(unit[:24, :24], cross, (((1,), (1,)), ((), ())), precision=lax.Precision.HIGHEST)
     left = jnp.concatenate(
-        [jnp.concatenate([g[:, 0:24], g[:, 96:120], blank], 1), jnp.concatenate([g[:, 64:88], g[:, 32:56], blank], 1)], 0
+        [jnp.concatenate([first, turned, blank], 1), jnp.concatenate([cross, second, blank], 1)], 0
     )
-    table = jnp.concatenate([left, (row == col).astype(F32)], 1)
+    table = jnp.concatenate([left, unit], 1)
     rows = lax.broadcasted_iota(jnp.int32, (48, 128), 0)
     for k in range(0, 48, 2):
         one = jnp.broadcast_to(table[:, k : k + 1], (48, 128))

time: 107 us -> 106 us (level)
  no operation moved by 1% of the time
where the time goes in v6:
time: 106 us
  Pallas kernels  106 us (100%)
    pallas_call x1, Pallas kernels, filter_call(): pl.pallas_call(filter_kernel, out_shape=(jax.ShapeDtypeStruct(chunk, F32)...  99.1 us
    pallas_call x1, Pallas kernels, rotate_call(): pl.pallas_call(rotate_kernel, out_shape=jax.ShapeDtypeStruct((24, 216, 12...  7.09 us

profile of v6, /device:TPU:2, one launch (start us, length us, event | category | flops | bytes accessed | tf_op | source)
XLA Modules:
  0.0 106.2 jit_solution(12529857469919850847)
XLA Ops:
  0.0 99.1 %filter.1 = (f32[3,12,8,2304]{3,2,1,0:T(8,128)}, f32[3,12,8,2304]{3,2,1,0:T(8,128)}, f32[16,128]{1,0:T(8,128)}) custom-call(f32[5184,128]{1,0:T(8,128)} %bitcast.3, f32[216,128]{1,0:T(8,128)} %bitcast.4, bf16[3,1280,256]{2,1,0:T(8,128)(2,1)} %constant.6.clone.wh_hbm, bf16[3,1280,256]{2,1,0:T(8,128)(2,1)} %constant.7.clone.wl_hbm, ...), custom_call_target="tpu_custom_call" | custom-call | tf_op jit(solution)/shard_map/filter/pallas_call | solution.py:527
  99.1 7.1 %rotate.1 = f32[24,216,128]{2,1,0:T(8,128)} custom-call(f32[3,12,8,2304]{3,2,1,0:T(8,128)} %get-tuple-element.8.low, f32[3,12,8,2304]{3,2,1,0:T(8,128)} %get-tuple-element.9.high, f32[16,128]{1,0:T(8,128)} %get-tuple-element.10.gram), custom_call_target="tpu_custom_call" | custom-call | tf_op jit(solution)/shard_map/rotate/pallas_call | solution.py:656

commit v7 on v6

--- a/solution.py
+++ b/solution.py
@@ -102,7 +102,8 @@
 
     stages = [
         [across(k // 2, k % 2, 0, 0, 0) for k in range(1, 8)],
-        [across(0, 0, k // 4, k // 2 % 2, k % 2) for k in range(1, 16)],
+        [across(0, 0, k, 0, 0) for k in range(1, 4)],
+        [across(0, 0, 0, k % 2, k // 2) for k in range(1, 4)],
     ]
     partners = [partner for stage in stages for partner in stage]
     barrier = pltpu.get_barrier_semaphore()
@@ -334,6 +335,16 @@
                 prepare(chunk, group(i))
                 send(chunk, group(i), 4, 2)
 
+    def fil_out(chunk):
+        return pltpu.make_async_copy(fil.at[chunk], f_hbm.at[chunk], out_sem.at[chunk])
+
+    def oth_out(chunk):
+        return pltpu.make_async_copy(oth.at[chunk], fo_hbm.at[chunk], out_sem.at[3 + chunk])
+
+    def last_out(half):
+        layers = pl.ds(6 * half, 6)
+        return pltpu.make_async_copy(oth.at[2, layers], fo_hbm.at[2, layers], out_sem.at[5 + half])
+
     acc[...] = jnp.zeros_like(acc)
     loads[0].wait()
     loads[1].wait()
@@ -418,7 +429,7 @@
             def _():
                 own_products(m)
 
-        pltpu.make_async_copy(fil.at[chunk], f_hbm.at[chunk], out_sem.at[chunk]).start()
+        fil_out(chunk).start()
 
     def cross_products(m):
         for chunk in range(3):
@@ -450,6 +461,64 @@
         + pltpu.roll(cross[:16], 112, 1)
         + jnp.concatenate([jnp.where(band == 0, tail, 0.0) + pltpu.roll(cross[16:], 32, 1), jnp.where(band == 0, 0.0, tail)], 0)
     )
+
+    def settle_early():
+        @pl.when(band == 1)
+        def _():
+            last_out(1).start()
+
+            @pl.loop(0, 2)
+            def _(chunk):
+                for m in range(3):
+                    band_copy(chunk, m, 0).wait_recv()
+                oth_out(chunk).start()
+
+        @pl.loop(0, 6)
+        def _(slot):
+            for m in range(3):
+                for copy in copies(slot, m):
+                    copy.wait_send()
+            for face in range(2):
+
+                def wait_outer():
+                    for copy in y_copies(slot, face, odds[0]):
+                        copy.wait_send()
+
+                for copy in y_copies(slot, face, 1 - odds[0]):
+                    copy.wait_send()
+                for_outer(face, wait_outer)
+            for copy in forward_copies(slot, 0):
+                copy.wait_send()
+
+    def settle_late():
+        @pl.loop(0, 2)
+        def _(chunk):
+            for m in range(3):
+                band_copy(chunk, m, 1 - band).wait_send()
+
+            @pl.when(band == 0)
+            def _():
+                for m in range(3):
+                    band_copy(chunk, m, 0).wait_send()
+
+            @pl.when(band == 1)
+            def _():
+                oth_out(chunk).wait()
+
+        for chunk in range(3):
+            fil_out(chunk).wait()
+
+        @pl.when(band == 0)
+        def _():
+            for m in range(3):
+                band_copy(2, m, 0).wait_send()
+
+        @pl.when(band == 1)
+        def _():
+            for m in range(3):
+                band_copy(2, m, 0).wait_recv()
+            last_out(0).start()
+            last_out(1).wait()
 
     index = 0
     for number, stage in enumerate(stages):
@@ -464,12 +533,13 @@
             index += 1
         for move in moves:
             move.start()
+        (settle_early, lambda: None, settle_late)[number]()
         for move in moves:
             move.wait_recv()
         terms = [part[number]] + [got[index - len(stage) + k] for k in range(len(stage))]
         while len(terms) > 1:
             terms = [a + b for a, b in zip(terms[::2], terms[1::2])]
-        if number < 1:
+        if number < 2:
             part[number + 1] = terms[0]
         else:
             gram[...] = terms[0]
@@ -478,44 +548,7 @@
 
     @pl.when(band == 1)
     def _():
-        @pl.loop(0, 3)
-        def _(chunk):
-            for m in range(3):
-                band_copy(chunk, m, 0).wait_recv()
-            copy = pltpu.make_async_copy(oth.at[chunk], fo_hbm.at[chunk], out_sem.at[3 + chunk])
-            copy.start()
-            copy.wait()
-
-    @pl.loop(0, 6)
-    def _(slot):
-        for m in range(3):
-            for copy in copies(slot, m):
-                copy.wait_send()
-        for face in range(2):
-
-            def wait_outer():
-                for copy in y_copies(slot, face, odds[0]):
-                    copy.wait_send()
-
-            for copy in y_copies(slot, face, 1 - odds[0]):
-                copy.wait_send()
-            for_outer(face, wait_outer)
-        for copy in forward_copies(slot, 0):
-            copy.wait_send()
-
-    @pl.loop(0, 3)
-    def _(chunk):
-        @pl.when(chunk < 2)
-        def _():
-            for m in range(3):
-                band_copy(chunk, m, 1 - band).wait_send()
-
-        @pl.when(band == 0)
-        def _():
-            for m in range(3):
-                band_copy(chunk, m, 0).wait_send()
-
-        pltpu.make_async_copy(fil.at[chunk], f_hbm.at[chunk], out_sem.at[chunk]).wait()
+        last_out(0).wait()
 
 
 def filter_call(lines, pot):
@@ -556,10 +589,10 @@
             vm(chunk, F32),
             vm(chunk, F32),
             vm((24, 128), F32),
-            vm((2, 16, 128), F32),
-            vm((22, 16, 128), F32),
+            vm((3, 16, 128), F32),
+            vm((13, 16, 128), F32),
             pltpu.SemaphoreType.DMA((7,)),
-            pltpu.SemaphoreType.DMA((6,)),
+            pltpu.SemaphoreType.DMA((7,)),
             pltpu.SemaphoreType.DMA((6, 3, 6)),
             pltpu.SemaphoreType.DMA((6, 3, 6)),
             pltpu.SemaphoreType.DMA((6, 2, 2, 2)),
@@ -567,8 +600,8 @@
             pltpu.SemaphoreType.DMA((6, 2)),
             pltpu.SemaphoreType.DMA((3, 3, 2)),
             pltpu.SemaphoreType.DMA((3, 3, 2)),
-            pltpu.SemaphoreType.DMA((22,)),
-            pltpu.SemaphoreType.DMA((22,)),
+            pltpu.SemaphoreType.DMA((13,)),
+            pltpu.SemaphoreType.DMA((13,)),
         ],
         compiler_params=pltpu.CompilerParams(collective_id=0, has_side_effects=True, vmem_limit_bytes=56 << 20),
         name="filter",

time: 106 us -> 103 us (0.972)
  Pallas kernels: 106 us -> 103 us
    pallas_call x1, Pallas kernels: 99.1 us -> 95.6 us  [filter_call(): pl.pallas_call(filter_kernel, out_shape=(jax.ShapeDtypeStruct(chunk, F32)...]
where the time goes in v7:
time: 103 us
  Pallas kernels  103 us (100%)
    pallas_call x1, Pallas kernels, filter_call(): pl.pallas_call(filter_kernel, out_shape=(jax.ShapeDtypeStruct(chunk, F32)...  95.6 us
    pallas_call x1, Pallas kernels, rotate_call(): pl.pallas_call(rotate_kernel, out_shape=jax.ShapeDtypeStruct((24, 216, 12...  7.09 us

profile of v7, /device:TPU:2, one launch (start us, length us, event | category | flops | bytes accessed | tf_op | source)
XLA Modules:
  0.0 102.7 jit_solution(18350247742097678849)
XLA Ops:
  0.0 95.6 %filter.1 = (f32[3,12,8,2304]{3,2,1,0:T(8,128)}, f32[3,12,8,2304]{3,2,1,0:T(8,128)}, f32[16,128]{1,0:T(8,128)}) custom-call(f32[5184,128]{1,0:T(8,128)} %bitcast.3, f32[216,128]{1,0:T(8,128)} %bitcast.4, bf16[3,1280,256]{2,1,0:T(8,128)(2,1)} %constant.6.clone.wh_hbm, bf16[3,1280,256]{2,1,0:T(8,128)(2,1)} %constant.7.clone.wl_hbm, ...), custom_call_target="tpu_custom_call" | custom-call | tf_op jit(solution)/shard_map/filter/pallas_call | solution.py:560
  95.6 7.1 %rotate.1 = f32[24,216,128]{2,1,0:T(8,128)} custom-call(f32[3,12,8,2304]{3,2,1,0:T(8,128)} %get-tuple-element.8.low, f32[3,12,8,2304]{3,2,1,0:T(8,128)} %get-tuple-element.9.high, f32[16,128]{1,0:T(8,128)} %get-tuple-element.10.gram), custom_call_target="tpu_custom_call" | custom-call | tf_op jit(solution)/shard_map/rotate/pallas_call | solution.py:689

commit v8 on v7

--- a/solution.py
+++ b/solution.py
@@ -660,8 +660,9 @@
         mh, ml = split(matrix)
         left = jnp.concatenate([jnp.concatenate([mh, mh], 1), jnp.concatenate([ml, jnp.zeros_like(ml)], 1)], 0)
         for x in range(CX):
-            for load in loads(x)[: len(sources)]:
-                load.wait()
+            for ready in range(x, x + 4) if x % 4 == 0 else ():
+                for load in loads(ready)[: len(sources)]:
+                    load.wait()
             v = [source[:, x].reshape(24, CYZ) for source in sources]
             vh, vl = split(jnp.concatenate(v, 0) if len(v) > 1 else v[0])
             made = dot(left, jnp.concatenate([vh, vl], 0))

time: 103 us -> 102 us (level)
  Pallas kernels: 103 us -> 101 us
    pallas_call x1, Pallas kernels: 7.09 us -> 5.72 us  [rotate_call(): pl.pallas_call(rotate_kernel, out_shape=jax.ShapeDtypeStruct((24, 216, 12...]
where the time goes in v8:
time: 102 us; the launch traced here: 101 us
  Pallas kernels  101 us (99%)
    pallas_call x1, Pallas kernels, filter_call(): pl.pallas_call(filter_kernel, out_shape=(jax.ShapeDtypeStruct(chunk, F32)...  95.6 us
    pallas_call x1, Pallas kernels, rotate_call(): pl.pallas_call(rotate_kernel, out_shape=jax.ShapeDtypeStruct((24, 216, 12...  5.72 us

profile of v8, /device:TPU:2, one launch (start us, length us, event | category | flops | bytes accessed | tf_op | source)
XLA Modules:
  0.0 101.3 jit_solution(2895988448591593115)
XLA Ops:
  0.0 95.6 %filter.1 = (f32[3,12,8,2304]{3,2,1,0:T(8,128)}, f32[3,12,8,2304]{3,2,1,0:T(8,128)}, f32[16,128]{1,0:T(8,128)}) custom-call(f32[5184,128]{1,0:T(8,128)} %bitcast.3, f32[216,128]{1,0:T(8,128)} %bitcast.4, bf16[3,1280,256]{2,1,0:T(8,128)(2,1)} %constant.6.clone.wh_hbm, bf16[3,1280,256]{2,1,0:T(8,128)(2,1)} %constant.7.clone.wl_hbm, ...), custom_call_target="tpu_custom_call" | custom-call | tf_op jit(solution)/shard_map/filter/pallas_call | solution.py:560
  95.6 5.7 %rotate.1 = f32[24,216,128]{2,1,0:T(8,128)} custom-call(f32[3,12,8,2304]{3,2,1,0:T(8,128)} %get-tuple-element.8.low, f32[3,12,8,2304]{3,2,1,0:T(8,128)} %get-tuple-element.9.high, f32[16,128]{1,0:T(8,128)} %get-tuple-element.10.gram), custom_call_target="tpu_custom_call" | custom-call | tf_op jit(solution)/shard_map/rotate/pallas_call | solution.py:690
